TPU v7x, 32 devices: a whole 2x2x4 slice. The times are simulated.
32 devices in a mesh: ctx: 4 (over z), fsdp: 4 (over y, x), replica: 2 (over core).
Axes of the slice: x: 2, y: 2, z: 4, core: 2. Of those that a mesh axis runs over, the one named last changes fastest.
Arguments:
- tokens: bfloat16 [8, 512, 1024], P(('fsdp', 'replica'), 'ctx'), may hold values from -6 to 6
- output_gradient: bfloat16 [8, 512, 1024], P(('fsdp', 'replica'), 'ctx'), may hold values from -6 to 6
- segment_ids: int32 [8, 512], P(('fsdp', 'replica')), may hold values from 0 to 2, as said below
- row_fill: int32 [8], P(('fsdp', 'replica')), may hold values from 256 to 512, as said below
- w_qkv: float32 [1024, 3072], P(('ctx', 'fsdp')), may hold values from -0.1875 to 0.1875
- w_attn_out: float32 [1024, 1024], P(('ctx', 'fsdp')), may hold values from -0.5 to 0.5
- w_up: float32 [1024, 4096], P(('ctx', 'fsdp')), may hold values from -0.1875 to 0.1875
- w_down: float32 [4096, 1024], P(('ctx', 'fsdp')), may hold values from -0.09375 to 0.09375
- vectors: float32 [13312], P(('ctx', 'fsdp')), may hold values from -0.5 to 1.4, as said below
- momentum_qkv_weight: float32 [1024, 3072], P(('ctx', 'fsdp')), may hold values from -80 to 80
- momentum_attn_output: float32 [1024, 1024], P(('ctx', 'fsdp')), may hold values from -16 to 16
- momentum_up_weight: float32 [1024, 4096], P(('ctx', 'fsdp')), may hold values from -10 to 10
- momentum_down_weight: float32 [4096, 1024], P(('ctx', 'fsdp')), may hold values from -24 to 24
- momentum_vector_rows: float32 [13312], P(('ctx', 'fsdp')), may hold values from -40 to 40
- second_qkv: float32 [1024, 3072], P(('ctx', 'fsdp')), may hold values from 860.16 to 3440.64
- second_attn_out: float32 [1024, 1024], P(('ctx', 'fsdp')), may hold values from 34.4064 to 139.264
- second_up: float32 [1024, 4096], P(('ctx', 'fsdp')), may hold values from 12.94336 to 51.6096
- second_down: float32 [4096, 1024], P(('ctx', 'fsdp')), may hold values from 64.7168 to 258.048
- second_vectors: float32 [13312], P(('ctx', 'fsdp')), may hold values from 215.4496 to 860.16
Outputs:
- block_out: bfloat16 [8, 512, 1024], P(('fsdp', 'replica'), 'ctx')
- tokens_grad: float32 [8, 512, 1024], P(('fsdp', 'replica'), 'ctx')
- next_qkv: float32 [1024, 3072], P(('ctx', 'fsdp'))
- next_attn_out: float32 [1024, 1024], P(('ctx', 'fsdp'))
- next_up: float32 [1024, 4096], P(('ctx', 'fsdp'))
- next_down: float32 [4096, 1024], P(('ctx', 'fsdp'))
- next_vectors: float32 [13312], P(('ctx', 'fsdp'))
- next_first_qkv: float32 [1024, 3072], P(('ctx', 'fsdp'))
- next_first_attn_out: float32 [1024, 1024], P(('ctx', 'fsdp'))
- next_first_up: float32 [1024, 4096], P(('ctx', 'fsdp'))
- next_first_down: float32 [4096, 1024], P(('ctx', 'fsdp'))
- next_first_vectors: float32 [13312], P(('ctx', 'fsdp'))
- next_second_qkv: float32 [1024, 3072], P(('ctx', 'fsdp'))
- next_second_attn_out: float32 [1024, 1024], P(('ctx', 'fsdp'))
- next_second_up: float32 [1024, 4096], P(('ctx', 'fsdp'))
- next_second_down: float32 [4096, 1024], P(('ctx', 'fsdp'))
- next_second_vectors: float32 [13312], P(('ctx', 'fsdp'))
Inputs may be any that keep to these rules, and one draw needn't show every extreme that they name: `segment_ids`: each row holds three documents numbered 0, 1, 2 in order of position; document 0 ends within the first eighth of the row and document 2 begins within the last eighth. `row_fill`: some row is full and some row is live on exactly half of its positions. `vectors`: entries of g1 and g2 lie in 0.6 to 1.4; the other entries lie in -0.5 to 0.5.
All inputs are finite; a program needn't handle non-finite values.
Results may differ from a plain program's by a relative error of at most 0.012.
Values may be sent and summed in bfloat16 or wider, within the bound.
A program may use at most 256 MiB of HBM per device.

v0:
```python
import jax
import jax.numpy as jnp
from jax import lax
from jax.sharding import PartitionSpec as P

MODEL_WIDTH = 1024
HEADS = 16
HEAD_DIM = 64
HIDDEN_UNITS = 4096
STEP = 10


norm_eps = 1e-05
score_scale = 0.125
masked_score = -1e30
gelu_coef = 0.7978845608028654
beta_one = 0.9
beta_two = 0.95
adam_eps = 1e-08


def layer_norm(inputs, scale_vec, shift_vec):
    centre = inputs - jnp.mean(inputs, axis=-1, keepdims=True)
    spread = jnp.mean(centre * centre, axis=-1, keepdims=True)
    return centre * lax.rsqrt(spread + norm_eps) * scale_vec + shift_vec


def gelu_tanh(points):
    return (
        0.5 * points * (1.0 + jnp.tanh(gelu_coef * (points + 0.044715 * points * points * points)))
    )


def alibi_slopes(count_heads):
    return jnp.power(2.0, -8.0 * (jnp.arange(count_heads, dtype=jnp.float32) + 1.0) / count_heads)


def split_small(vector_all):
    bounds = [
        0,
        MODEL_WIDTH,
        2 * MODEL_WIDTH,
        5 * MODEL_WIDTH,
        6 * MODEL_WIDTH,
        7 * MODEL_WIDTH,
        8 * MODEL_WIDTH,
        8 * MODEL_WIDTH + HIDDEN_UNITS,
        9 * MODEL_WIDTH + HIDDEN_UNITS,
    ]
    return tuple(
        (vector_all[low_end:high_end] for low_end, high_end in zip(bounds[:-1], bounds[1:]))
    )


def outer_sum(left_mat, right_mat):
    return lax.dot_general(
        left_mat, right_mat, (((0,), (0,)), ((), ())), preferred_element_type=jnp.float32
    )


def times_trans(left_mat, right_mat):
    return lax.dot_general(
        left_mat, right_mat, (((1,), (1,)), ((), ())), preferred_element_type=jnp.float32
    )


def attention_scores(heads_q, heads_k, alibi_bias, allowed):
    scores = (
        jnp.einsum("qhd,khd->hqk", heads_q, heads_k, preferred_element_type=jnp.float32)
        * score_scale
        + alibi_bias
    )
    return jnp.where(allowed[None], scores, masked_score)


def adamw_update(weight, gradient, first_mom, second, step_rate, decay_rate):
    first_new = beta_one * first_mom + (1.0 - beta_one) * gradient
    second_new = beta_two * second + (1.0 - beta_two) * gradient * gradient
    first_hat = first_new / (1.0 - beta_one**STEP)
    second_hat = second_new / (1.0 - beta_two**STEP)
    weight_new = weight - step_rate * (
        first_hat / (jnp.sqrt(second_hat) + adam_eps) + decay_rate * weight
    )
    return (weight_new, first_new, second_new)


def shards(
    tokens,
    output_gradient,
    segment_ids,
    row_fill,
    w_qkv,
    w_attn_out,
    w_up,
    w_down,
    vectors,
    momentum_qkv_weight,
    momentum_attn_output,
    momentum_up_weight,
    momentum_down_weight,
    momentum_vector_rows,
    second_qkv,
    second_attn_out,
    second_up,
    second_down,
    second_vectors,
):
    low_qkv = w_qkv.astype(jnp.bfloat16)
    low_out = w_attn_out.astype(jnp.bfloat16)
    low_up = w_up.astype(jnp.bfloat16)
    low_down = w_down.astype(jnp.bfloat16)
    low_vec = vectors.astype(jnp.bfloat16)
    mat_qkv, mat_out, mat_up, mat_down, vec_full = (
        lax.all_gather(low_qkv, ("ctx", "fsdp"), axis=0, tiled=True),
        lax.all_gather(low_out, ("ctx", "fsdp"), axis=0, tiled=True),
        lax.all_gather(low_up, ("ctx", "fsdp"), axis=0, tiled=True),
        lax.all_gather(low_down, ("ctx", "fsdp"), axis=0, tiled=True),
        lax.all_gather(low_vec, ("ctx", "fsdp"), axis=0, tiled=True),
    )
    gain_one, shift_one, bias_qkv, bias_out, gain_two, shift_two, bias_up, bias_down = split_small(
        vec_full.astype(jnp.float32)
    )
    row_vals = tokens[0].astype(jnp.float32)
    length = row_vals.shape[0]
    first_pos = lax.axis_index("ctx") * length
    place_q = first_pos + jnp.arange(length, dtype=jnp.int32)
    seg_row = segment_ids[0]
    full_len = seg_row.shape[0]
    place_k = jnp.arange(full_len, dtype=jnp.int32)
    seg_q = lax.dynamic_slice_in_dim(seg_row, first_pos, length)
    allowed = (place_k[None, :] <= place_q[:, None]) & (seg_q[:, None] == seg_row[None, :])
    distance = (place_q[:, None] - place_k[None, :]).astype(jnp.float32)
    alibi_bias = -alibi_slopes(HEADS)[:, None, None] * distance[None, :, :]
    normed_one, ln_one_pull = jax.vjp(layer_norm, row_vals, gain_one, shift_one)
    hidden_one = normed_one.astype(jnp.bfloat16)
    qkv_low = (jnp.dot(hidden_one, mat_qkv, preferred_element_type=jnp.float32) + bias_qkv).astype(
        jnp.bfloat16
    )
    queries = qkv_low[:, :MODEL_WIDTH]
    keys_low = qkv_low[:, MODEL_WIDTH : 2 * MODEL_WIDTH]
    values_low = qkv_low[:, 2 * MODEL_WIDTH :]
    key_all, value_all = (
        lax.all_gather(keys_low, "ctx", axis=0, tiled=True),
        lax.all_gather(values_low, "ctx", axis=0, tiled=True),
    )
    heads_q = queries.reshape(length, HEADS, HEAD_DIM)
    heads_k = key_all.reshape(full_len, HEADS, HEAD_DIM)
    heads_v = value_all.reshape(full_len, HEADS, HEAD_DIM)
    scores = attention_scores(heads_q, heads_k, alibi_bias, allowed)
    row_max = jnp.max(scores, axis=-1, keepdims=True)
    exp_scores = jnp.exp(scores - row_max)
    row_sum = jnp.sum(exp_scores, axis=-1, keepdims=True)
    log_sum = row_max + jnp.log(row_sum)
    probs_low = (exp_scores / row_sum).astype(jnp.bfloat16)
    attn_mix = jnp.einsum("hqk,khd->qhd", probs_low, heads_v, preferred_element_type=jnp.float32)
    attn_mix = attn_mix.reshape(length, MODEL_WIDTH).astype(jnp.bfloat16)
    attn_out = jnp.dot(attn_mix, mat_out, preferred_element_type=jnp.float32) + bias_out
    resid_one = row_vals + attn_out
    normed_two, ln_two_pull = jax.vjp(layer_norm, resid_one, gain_two, shift_two)
    hidden_two = normed_two.astype(jnp.bfloat16)
    up_pre = jnp.dot(hidden_two, mat_up, preferred_element_type=jnp.float32) + bias_up
    act_out, gelu_pull = jax.vjp(gelu_tanh, up_pre)
    act_low = act_out.astype(jnp.bfloat16)
    down_out = jnp.dot(act_low, mat_down, preferred_element_type=jnp.float32) + bias_down
    block_out = (resid_one + down_out).astype(jnp.bfloat16)[None]
    live_rows = place_q < row_fill[0]
    grad_low = jnp.where(live_rows[:, None], output_gradient[0], jnp.zeros_like(output_gradient[0]))
    grad_vals = grad_low.astype(jnp.float32)
    grad_bias_down = jnp.sum(grad_vals, axis=0)
    grad_act = times_trans(grad_low, mat_down)
    grad_up_low = gelu_pull(grad_act)[0].astype(jnp.bfloat16)
    grad_bias_up = jnp.sum(grad_up_low.astype(jnp.float32), axis=0)
    grad_normed_two = times_trans(grad_up_low, mat_up)
    grad_resid_ln, grad_gain_two, grad_shift_two = ln_two_pull(grad_normed_two)
    grad_resid = grad_vals + grad_resid_ln
    grad_attn = grad_resid.astype(jnp.bfloat16)
    grad_bias_out = jnp.sum(grad_attn.astype(jnp.float32), axis=0)
    grad_mixed = (
        times_trans(grad_attn, mat_out).astype(jnp.bfloat16).reshape(length, HEADS, HEAD_DIM)
    )
    scores_again = attention_scores(heads_q, heads_k, alibi_bias, allowed)
    probs_vals = jnp.exp(scores_again - log_sum)
    probs_again = probs_vals.astype(jnp.bfloat16)
    grad_value_part = jnp.einsum(
        "hqk,qhd->khd", probs_again, grad_mixed, preferred_element_type=jnp.float32
    )
    grad_probs = jnp.einsum("qhd,khd->hqk", grad_mixed, heads_v, preferred_element_type=jnp.float32)
    grad_scores = probs_vals * (
        grad_probs - jnp.sum(probs_vals * grad_probs, axis=-1, keepdims=True)
    )
    grad_scores_low = grad_scores.astype(jnp.bfloat16)
    grad_query = (
        jnp.einsum("hqk,khd->qhd", grad_scores_low, heads_k, preferred_element_type=jnp.float32)
        * score_scale
    )
    grad_key_part = (
        jnp.einsum("hqk,qhd->khd", grad_scores_low, heads_q, preferred_element_type=jnp.float32)
        * score_scale
    )
    grad_key, grad_value = (
        lax.psum_scatter(
            grad_key_part.reshape(full_len, MODEL_WIDTH), "ctx", scatter_dimension=0, tiled=True
        ),
        lax.psum_scatter(
            grad_value_part.reshape(full_len, MODEL_WIDTH), "ctx", scatter_dimension=0, tiled=True
        ),
    )
    grad_qkv_low = jnp.concatenate(
        [grad_query.reshape(length, MODEL_WIDTH), grad_key, grad_value], axis=1
    ).astype(jnp.bfloat16)
    grad_bias_qkv = jnp.sum(grad_qkv_low.astype(jnp.float32), axis=0)
    grad_normed_one = times_trans(grad_qkv_low, mat_qkv)
    grad_rows_ln, grad_gain_one, grad_shift_one = ln_one_pull(grad_normed_one)
    tokens_grad = (grad_resid + grad_rows_ln)[None]
    grad_vec = jnp.concatenate(
        [
            grad_gain_one,
            grad_shift_one,
            grad_bias_qkv,
            grad_bias_out,
            grad_gain_two,
            grad_shift_two,
            grad_bias_up,
            grad_bias_down,
        ]
    )
    count = lax.axis_size(("ctx", "fsdp")) * 1
    qkv_part = outer_sum(hidden_one, grad_qkv_low)
    out_part = outer_sum(attn_mix, grad_attn)
    up_part = outer_sum(hidden_two, grad_up_low)
    down_part = outer_sum(act_low, grad_low)
    shard_packed = lax.psum_scatter(
        jnp.concatenate(
            [
                qkv_part.reshape(count, -1),
                out_part.reshape(count, -1),
                up_part.reshape(count, -1),
                down_part.reshape(count, -1),
                grad_vec.reshape(count, -1),
            ],
            axis=1,
        ),
        ("ctx", "fsdp"),
        scatter_dimension=0,
        tiled=True,
    )
    total_packed = lax.psum(shard_packed, "replica").reshape(-1)
    sizes_in_order = [w_qkv.size, w_attn_out.size, w_up.size, w_down.size, vectors.size]
    offsets = [0]
    for entry_count in sizes_in_order:
        offsets.append(offsets[-1] + entry_count)
    total_qkv = total_packed[offsets[0] : offsets[1]].reshape(w_qkv.shape)
    total_out = total_packed[offsets[1] : offsets[2]].reshape(w_attn_out.shape)
    total_up = total_packed[offsets[2] : offsets[3]].reshape(w_up.shape)
    total_down = total_packed[offsets[3] : offsets[4]].reshape(w_down.shape)
    total_vec = total_packed[offsets[4] : offsets[5]]
    new_qkv, mom_qkv, sec_qkv = adamw_update(
        w_qkv, total_qkv, momentum_qkv_weight, second_qkv, 0.05, 0.1
    )
    new_out, mom_out, sec_out = adamw_update(
        w_attn_out, total_out, momentum_attn_output, second_attn_out, 0.05, 0.1
    )
    new_up, mom_up, sec_up = adamw_update(w_up, total_up, momentum_up_weight, second_up, 0.05, 0.1)
    new_down, mom_down, sec_down = adamw_update(
        w_down, total_down, momentum_down_weight, second_down, 0.05, 0.1
    )
    new_vec, mom_vec, sec_vec = adamw_update(
        vectors, total_vec, momentum_vector_rows, second_vectors, 0.6, 0.0
    )
    return (
        block_out,
        tokens_grad,
        new_qkv,
        new_out,
        new_up,
        new_down,
        new_vec,
        mom_qkv,
        mom_out,
        mom_up,
        mom_down,
        mom_vec,
        sec_qkv,
        sec_out,
        sec_up,
        sec_down,
        sec_vec,
    )


def solution(mesh):
    placed = (
        P(("fsdp", "replica"), "ctx", None),
        P(("fsdp", "replica"), "ctx", None),
        P(("fsdp", "replica"), None),
        P(("fsdp", "replica")),
        P(("ctx", "fsdp"), None),
        P(("ctx", "fsdp"), None),
        P(("ctx", "fsdp"), None),
        P(("ctx", "fsdp"), None),
        P(("ctx", "fsdp")),
        P(("ctx", "fsdp"), None),
        P(("ctx", "fsdp"), None),
        P(("ctx", "fsdp"), None),
        P(("ctx", "fsdp"), None),
        P(("ctx", "fsdp")),
        P(("ctx", "fsdp"), None),
        P(("ctx", "fsdp"), None),
        P(("ctx", "fsdp"), None),
        P(("ctx", "fsdp"), None),
        P(("ctx", "fsdp")),
    )
    return jax.shard_map(
        shards,
        mesh=mesh,
        in_specs=placed,
        out_specs=(
            P(("fsdp", "replica"), "ctx", None),
            P(("fsdp", "replica"), "ctx", None),
            P(("ctx", "fsdp"), None),
            P(("ctx", "fsdp"), None),
            P(("ctx", "fsdp"), None),
            P(("ctx", "fsdp"), None),
            P(("ctx", "fsdp")),
            P(("ctx", "fsdp"), None),
            P(("ctx", "fsdp"), None),
            P(("ctx", "fsdp"), None),
            P(("ctx", "fsdp"), None),
            P(("ctx", "fsdp")),
            P(("ctx", "fsdp"), None),
            P(("ctx", "fsdp"), None),
            P(("ctx", "fsdp"), None),
            P(("ctx", "fsdp"), None),
            P(("ctx", "fsdp")),
        ),
        check_vma=False,
    )
```

profile of v0, /device:TPU:0, one launch (start us, length us, event | category | flops | bytes accessed | tf_op | source)
XLA Modules:
  0.0 1983.3 jit_solution(6162493907623544710)
XLA Ops:
  7.2 2.0 convert_element_type.91
  10.0 1.3 fusion.58
  12.2 80.2 %all-reduce = bf16[13312]{0:T(1024)(128)(2,1)S(1)} all-reduce(bf16[13312]{0:T(1024)(128)(2,1)S(1)} %dynamic-update-slice), channel_id=1, replica_groups=mesh['ctx'=4,'fsdp'=4,'replica'=2] {'ctx','fsdp'}, use_global_device_ids=true, to_apply=%add | all-reduce | flops 13312 | bytes 53248
  93.7 15.8 all-gather.7.cloned.1.call-done
  109.5 3.9 fusion.1
  118.9 22.0 %all-gather.9.cloned.1.call-done = bf16[512,1024]{1,0:T(8,128)(2,1)} async-done(((bf16[128,1024]{1,0:T(8,128)(2,1)}), bf16[512,1024]{1,0:T(8,128)(2,1)}) %all-gather.9.cloned.1.call-update) | async-done | bytes 1048592 | tf_op jit(solution)/shard_map/all_gather | solution.py:144
  140.9 1.5 copy.48
  142.5 28.1 %all-gather.11.cloned.1.call-done = bf16[512,1024]{1,0:T(8,128)(2,1)} async-done(((bf16[128,1024]{1,0:T(8,128)(2,1)}), bf16[512,1024]{1,0:T(8,128)(2,1)}) %all-gather.11.cloned.1.call-update) | async-done | bytes 1048592 | tf_op jit(solution)/shard_map/all_gather | solution.py:143
  170.5 1.5 copy.50
  175.3 1.7 fusion.17
  177.0 57.0 %all-gather.13.cloned.1.call-done = bf16[1024,1024]{1,0:T(8,128)(2,1)} async-done(((bf16[64,1024]{1,0:T(8,128)(2,1)}), bf16[1024,1024]{1,0:T(8,128)(2,1)}) %all-gather.13.cloned.1.call-update) | async-done | bytes 2097168 | tf_op jit(solution)/shard_map/all_gather | solution.py:115
  234.0 2.1 fusion.60
  236.3 112.3 %all-gather.15.cloned.1.call-done = bf16[1024,4096]{1,0:T(8,128)(2,1)} async-done(((bf16[64,4096]{1,0:T(8,128)(2,1)}), bf16[1024,4096]{1,0:T(8,128)(2,1)}) %all-gather.15.cloned.1.call-update) | async-done | bytes 8388624 | tf_op jit(solution)/shard_map/all_gather | solution.py:116
  348.7 4.8 convolution_add_fusion
  353.4 109.5 %all-gather.17.cloned.1.call-done = bf16[4096,1024]{1,0:T(8,128)(2,1)} async-done(((bf16[256,1024]{1,0:T(8,128)(2,1)}), bf16[4096,1024]{1,0:T(8,128)(2,1)}) %all-gather.17.cloned.1.call-update) | async-done | bytes 8388624 | tf_op jit(solution)/shard_map/all_gather | solution.py:117
  462.9 7.7 convert_reduce_fusion
  470.7 3.0 multiply_reduce_fusion.1
  475.4 1.5 convolution_convert_fusion
  478.1 4.5 fusion.9
  483.8 3.8 multiply_reduce_fusion
  488.6 1.8 convolution_multiply_fusion
  490.7 3.7 fusion.61
  494.4 3.9 reshape.270
  498.4 9.4 fusion.45
  507.8 16.2 reshape.271
  524.0 10.0 fusion.46
  534.0 16.7 reshape.272
  550.7 2.8 fusion.16
  554.6 15.8 reduce-scatter.3.cloned.1.call-done
  571.5 7.5 fusion.40
  579.3 5.1 fusion.48
  585.9 13.1 reshape.269
  599.0 10.0 constant_dynamic-update-slice_fusion.5
  609.2 4.6 constant_dynamic-update-slice_fusion.4
  613.7 13.2 constant_dynamic-update-slice_fusion.3
  627.7 1.4 slice-done.3
  629.1 6.0 constant_dynamic-update-slice_fusion.2
  635.7 1270.3 %all-reduce.7.cloned.1.call-done = f32[16,787264]{1,0:T(8,128)} async-done(((f32[16,787264]{1,0:T(8,128)}), f32[16,787264]{1,0:T(8,128)}) %all-reduce.7.cloned.1.call-update) | async-done | bytes 50384912
  1906.0 11.2 constant_dynamic-slice_fusion
  1917.2 1.6 copy-done.5
  1918.8 5.6 fusion.18
  1924.4 15.3 all-reduce.5.cloned.1.call-done
  1939.7 9.1 slice_reduce_fusion.2
  1949.9 1.6 slice_reduce_fusion.3
  1951.5 12.4 slice_reduce_fusion
  1964.3 3.8 multiply_subtract_fusion.2
  1969.6 2.2 multiply_subtract_fusion.1
  1972.6 2.3 multiply_subtract_fusion
  (155 shorter events, 26.2 us)
Async XLA Ops:
  7.2 86.3 %copy-start.3 = (bf16[1,128,1024]{2,1,0:T(8,128)(2,1)S(1)}, bf16[1,128,1024]{2,1,0:T(8,128)(2,1)}, u32[]{:S(2)}) copy-start(bf16[1,128,1024]{2,1,0:T(8,128)(2,1)} %param.19) | copy-start | bytes 786436
  7.2 102.3 %all-gather.7.cloned.1.call-start = ((), (), s32[]{:S(2)}) async-start(), calls=%async_computation.2 | async-start | bytes 6684672 | tf_op jit(solution)/shard_map/all_gather | solution.py:114
  9.2 131.7 %all-gather.9.cloned.1.call-start = ((), (), s32[]{:S(2)}) async-start(), calls=%async_computation.3 | async-start | bytes 1310720 | tf_op jit(solution)/shard_map/all_gather | solution.py:144
  109.5 5.6 copy-start.24
  113.4 2.4 copy-start.8
  113.5 3.4 copy-start.10
  114.3 56.2 %all-gather.11.cloned.1.call-start = ((), (), s32[]{:S(2)}) async-start(), calls=%async_computation.4 | async-start | bytes 1310720 | tf_op jit(solution)/shard_map/all_gather | solution.py:143
  115.1 118.9 %all-gather.13.cloned.1.call-start = ((), (), s32[]{:S(2)}) async-start(), calls=%async_computation.5 | async-start | bytes 2228224 | tf_op jit(solution)/shard_map/all_gather | solution.py:115
  115.8 2.7 copy-start.34
  115.8 232.8 %all-gather.15.cloned.1.call-start = ((), (), s32[]{:S(2)}) async-start(), calls=%async_computation.6 | async-start | bytes 8912896 | tf_op jit(solution)/shard_map/all_gather | solution.py:116
  116.8 346.1 %all-gather.17.cloned.1.call-start = ((), (), s32[]{:S(2)}) async-start(), calls=%async_computation.7 | async-start | bytes 8912896 | tf_op jit(solution)/shard_map/all_gather | solution.py:117
  117.7 435.8 %reduce-scatter.5.cloned.1.call-start = ((), (), s32[]{:S(2)}) async-start(), calls=%async_computation.9 | async-start | bytes 2621440 | tf_op jit(solution)/shard_map/reduce_scatter | solution.py:204
  118.9 53.1 %copy-start.26 = (bf16[128,1024]{0,1:T(8,128)(2,1)}, bf16[128,1024]{0,1:T(8,128)(2,1)S(1)}, u32[]{:S(2)}) copy-start(bf16[128,1024]{0,1:T(8,128)(2,1)S(1)} %copy.49) | copy-start | bytes 786436
  142.4 32.1 %copy-start.12 = (bf16[512,1024]{0,1:T(8,128)(2,1)}, bf16[512,1024]{0,1:T(8,128)(2,1)S(1)}, u32[]{:S(2)}) copy-start(bf16[512,1024]{0,1:T(8,128)(2,1)S(1)} %copy.48) | copy-start | bytes 3145732
  172.0 1.3 copy-start.14
  173.3 2.0 copy-start
  177.0 171.7 %copy-start.28 = (bf16[16,64,128]{2,1,0:T(8,128)(2,1)}, bf16[16,64,128]{2,1,0:T(8,128)(2,1)S(1)}, u32[]{:S(2)}) copy-start(bf16[16,64,128]{2,1,0:T(8,128)(2,1)S(1)} %fusion.17) | copy-start | bytes 786436
  348.7 114.3 %copy-start.15 = (bf16[1,128,1024]{2,1,0:T(8,128)(2,1)S(1)}, bf16[1,128,1024]{2,1,0:T(8,128)(2,1)}, u32[]{:S(2)}) copy-start(bf16[1,128,1024]{2,1,0:T(8,128)(2,1)} %param.20) | copy-start | bytes 786436
  353.4 117.2 %copy-start.4 = (f32[128,4096]{1,0:T(8,128)}, f32[128,4096]{1,0:T(8,128)S(1)}, u32[]{:S(2)}) copy-start(f32[128,4096]{1,0:T(8,128)S(1)} %convolution_add_fusion) | copy-start | bytes 6291460
  462.9 7.7 copy-start.2
  470.6 3.1 copy-start.7
  470.7 3.4 copy-start.16
  473.7 1.7 copy-start.6
  482.5 1.2 copy-start.13
  482.6 87.8 %reduce-scatter.3.cloned.1.call-start = ((), (), s32[]{:S(2)}) async-start(), calls=%async_computation.8 | async-start | bytes 2621440 | tf_op jit(solution)/shard_map/reduce_scatter | solution.py:201
  483.8 3.8 copy-start.1
  487.6 1.0 copy-start.27
  490.4 1415.6 %all-reduce.7.cloned.1.call-start = ((), (), s32[]{:S(2)}) async-start(), calls=%async_computation.11 | async-start | bytes 100777984
  571.5 7.5 copy-start.19
  579.3 5.5 copy-start.17
  609.2 17.7 slice-start
  613.7 13.2 slice-start.1
  613.7 13.9 slice-start.2
  613.7 15.3 slice-start.3
  635.7 1304.1 %all-reduce.5.cloned.1.call-start = ((), (), s32[]{:S(2)}) async-start(), calls=%async_computation.10 | async-start | bytes 6298624 | tf_op jit(solution)/shard_map/psum | solution.py:247
  1917.2 1.6 copy-start.5
  1964.3 3.8 copy-start.25
  1964.3 3.8 copy-start.29
  1964.3 3.8 copy-start.30
  1964.3 4.8 copy-start.20
  1964.3 4.8 copy-start.21
  1968.1 1.5 copy-start.9
  1969.6 2.2 copy-start.11
  1969.6 2.2 copy-start.22
  1969.6 3.0 copy-start.23
  1972.6 2.9 copy-start.31
  1972.6 2.9 copy-start.32
  1972.6 2.9 copy-start.33
  (1 other events, 0.7 us)
Sparse Core Ops, SparseCore 0:
  11.4 98.0 all-gather.6
  114.5 26.4 all-gather.8
  143.1 27.3 all-gather.10
  173.7 60.1 all-gather.12
  237.1 111.4 all-gather.14
  351.9 111.0 all-gather.16
  482.7 42.0 reduce-scatter.4
  527.2 43.1 reduce-scatter.2
  635.8 1270.1 all-reduce.6
  1917.3 22.3 all-reduce.4
where the time goes:
time: 1990 us; the launch traced here: 1980 us
  waiting for transfers between devices  1650 us (83%)
  local copies, waits for them, and re-layouts  136 us (7%)
  blocking collectives  80.2 us (4%)
  matrix products  80.2 us (4%)
  other arithmetic  23.2 us (1%)
    unnamed x11, waiting for transfers between devices  1270 us
    all_gather x1, waiting for transfers between devices, shards(): lax.all_gather(low_up, ('ctx', 'fsdp'), axis=0, tiled=True)  112 us
    all_gather x1, waiting for transfers between devices, shards(): lax.all_gather(low_down, ('ctx', 'fsdp'), axis=0, tiled=True)  109 us
    unnamed x1, blocking collectives  80.2 us
    all_gather x1, waiting for transfers between devices, shards(): lax.all_gather(low_out, ('ctx', 'fsdp'), axis=0, tiled=True)  57 us
    unnamed x93, local copies, waits for them, and re-layouts  54.7 us
  transfers between devices with their start and end apart: 10, of which 9 were waited for; matrix products, arithmetic and copies ran while one was open for 5% of the time, Pallas kernels for 0%

commit v1 on v0

v1 whole, which is shorter than its diff:
```python
import jax
import jax.numpy as jnp
from jax import lax
from jax.sharding import PartitionSpec as P

MODEL_WIDTH = 1024
HEADS = 16
HEAD_DIM = 64
HIDDEN_UNITS = 4096
STEP = 10


norm_eps = 1e-05
score_scale = 0.125
masked_score = -1e30
gelu_coef = 0.7978845608028654
beta_one = 0.9
beta_two = 0.95
adam_eps = 1e-08


def layer_norm(inputs, scale_vec, shift_vec):
    centre = inputs - jnp.mean(inputs, axis=-1, keepdims=True)
    spread = jnp.mean(centre * centre, axis=-1, keepdims=True)
    return centre * lax.rsqrt(spread + norm_eps) * scale_vec + shift_vec


def gelu_tanh(points):
    return (
        0.5 * points * (1.0 + jnp.tanh(gelu_coef * (points + 0.044715 * points * points * points)))
    )


def alibi_slopes(count_heads):
    return jnp.power(2.0, -8.0 * (jnp.arange(count_heads, dtype=jnp.float32) + 1.0) / count_heads)


def split_small(vector_all):
    bounds = [
        0,
        MODEL_WIDTH,
        2 * MODEL_WIDTH,
        5 * MODEL_WIDTH,
        6 * MODEL_WIDTH,
        7 * MODEL_WIDTH,
        8 * MODEL_WIDTH,
        8 * MODEL_WIDTH + HIDDEN_UNITS,
        9 * MODEL_WIDTH + HIDDEN_UNITS,
    ]
    return tuple(
        (vector_all[low_end:high_end] for low_end, high_end in zip(bounds[:-1], bounds[1:]))
    )


def outer_sum(left_mat, right_mat):
    return lax.dot_general(
        left_mat, right_mat, (((0,), (0,)), ((), ())), preferred_element_type=jnp.float32
    )


def times_trans(left_mat, right_mat):
    return lax.dot_general(
        left_mat, right_mat, (((1,), (1,)), ((), ())), preferred_element_type=jnp.float32
    )


def adamw_update(weight, gradient, first_mom, second, step_rate, decay_rate):
    first_new = beta_one * first_mom + (1.0 - beta_one) * gradient
    second_new = beta_two * second + (1.0 - beta_two) * gradient * gradient
    first_hat = first_new / (1.0 - beta_one**STEP)
    second_hat = second_new / (1.0 - beta_two**STEP)
    weight_new = weight - step_rate * (
        first_hat / (jnp.sqrt(second_hat) + adam_eps) + decay_rate * weight
    )
    return (weight_new, first_new, second_new)


def shards(
    tokens,
    output_gradient,
    segment_ids,
    row_fill,
    w_qkv,
    w_attn_out,
    w_up,
    w_down,
    vectors,
    momentum_qkv_weight,
    momentum_attn_output,
    momentum_up_weight,
    momentum_down_weight,
    momentum_vector_rows,
    second_qkv,
    second_attn_out,
    second_up,
    second_down,
    second_vectors,
):
    parts, group = lax.axis_size("ctx"), lax.axis_size("fsdp")
    own = lax.axis_index("ctx")
    block = MODEL_WIDTH // parts
    hid = HIDDEN_UNITS // parts
    heads = HEADS // parts
    rows_in, rows_out, vec_len = w_qkv.shape[0], w_attn_out.shape[0], vectors.shape[0]
    tall = parts * rows_in
    folds = tall // rows_out
    fold_wide = MODEL_WIDTH // folds
    wide_qkv = 3 * block
    tokens_loc, grads_loc = tokens[0], output_gradient[0]
    length = tokens_loc.shape[0]
    seg_row = segment_ids[0]
    full_len = seg_row.shape[0]
    place_all = jnp.arange(full_len, dtype=jnp.int32)
    live_all = place_all < row_fill[0]
    place_loc = own * length + jnp.arange(length, dtype=jnp.int32)
    live_loc = place_loc < row_fill[0]

    vec_pad = jnp.pad(vectors.astype(jnp.bfloat16)[None, :], ((0, 15), (0, MODEL_WIDTH - vec_len)))
    seq_pack = lax.all_gather(
        jnp.concatenate([tokens_loc, grads_loc, vec_pad], axis=0), "ctx", axis=0, tiled=False
    )
    rows_all = seq_pack[:, :length].reshape(full_len, MODEL_WIDTH).astype(jnp.float32)
    dy_all = seq_pack[:, length : 2 * length].reshape(full_len, MODEL_WIDTH)
    dy_all = jnp.where(live_all[:, None], dy_all, jnp.zeros_like(dy_all))
    vec_ctx = seq_pack[:, 2 * length]

    send = jnp.concatenate(
        [
            w_qkv.astype(jnp.bfloat16)
            .reshape(rows_in, 3, parts, block)
            .transpose(2, 0, 1, 3)
            .reshape(parts, rows_in, wide_qkv),
            w_up.astype(jnp.bfloat16).reshape(rows_in, parts, hid).transpose(1, 0, 2),
        ],
        axis=2,
    )
    cols = lax.all_to_all(send, "ctx", 0, 0).reshape(tall, wide_qkv + hid)
    low_out = w_attn_out.astype(jnp.bfloat16)
    out_fold = jnp.concatenate(
        [low_out[:, i * fold_wide : (i + 1) * fold_wide] for i in range(folds)], axis=0
    )
    wide = wide_qkv + hid + MODEL_WIDTH + fold_wide
    pack = jnp.concatenate([cols, w_down.astype(jnp.bfloat16), out_fold], axis=1)
    vec_rows = jnp.pad(vec_ctx, ((0, 16 - parts), (0, wide - MODEL_WIDTH)))
    full = lax.all_gather(jnp.concatenate([pack, vec_rows], axis=0), "fsdp", axis=0, tiled=False)
    mats = full[:, :tall]

    def columns_whole(part):
        return (
            part.reshape(group, parts, rows_in, -1)
            .transpose(1, 0, 2, 3)
            .reshape(parts * group * rows_in, -1)
        )

    mat_qkv = columns_whole(mats[:, :, :wide_qkv])
    mat_up = columns_whole(mats[:, :, wide_qkv : wide_qkv + hid])
    mat_down = mats[:, :, wide_qkv + hid : wide_qkv + hid + MODEL_WIDTH].reshape(hid, MODEL_WIDTH)
    mat_out = (
        mats[:, :, wide_qkv + hid + MODEL_WIDTH :]
        .reshape(group, folds, rows_out, fold_wide)
        .transpose(0, 2, 1, 3)
        .reshape(block, MODEL_WIDTH)
    )
    vec_full = full[:, tall : tall + parts, :vec_len].transpose(1, 0, 2).reshape(-1)
    gain_one, shift_one, bias_qkv, bias_out, gain_two, shift_two, bias_up, bias_down = split_small(
        vec_full.astype(jnp.float32)
    )
    bias_qkv_own = lax.dynamic_slice_in_dim(
        bias_qkv.reshape(3, MODEL_WIDTH), own * block, block, axis=1
    ).reshape(-1)
    bias_up_own = lax.dynamic_slice_in_dim(bias_up, own * hid, hid)

    normed_one = layer_norm(rows_all, gain_one, shift_one)
    hidden_one = normed_one.astype(jnp.bfloat16)
    qkv_low = (
        jnp.dot(hidden_one, mat_qkv, preferred_element_type=jnp.float32) + bias_qkv_own
    ).astype(jnp.bfloat16)
    heads_q = qkv_low[:, :block].reshape(full_len, heads, HEAD_DIM)
    heads_k = qkv_low[:, block : 2 * block].reshape(full_len, heads, HEAD_DIM)
    heads_v = qkv_low[:, 2 * block :].reshape(full_len, heads, HEAD_DIM)
    allowed = (place_all[None, :] <= place_all[:, None]) & (seg_row[:, None] == seg_row[None, :])
    distance = (place_all[:, None] - place_all[None, :]).astype(jnp.float32)
    slopes = lax.dynamic_slice_in_dim(alibi_slopes(HEADS), own * heads, heads)
    scores = (
        jnp.einsum("qhd,khd->hqk", heads_q, heads_k, preferred_element_type=jnp.float32)
        * score_scale
        - slopes[:, None, None] * distance[None]
    )
    scores = jnp.where(allowed[None], scores, masked_score)
    row_max = jnp.max(scores, axis=-1, keepdims=True)
    exp_scores = jnp.exp(scores - row_max)
    probs_vals = exp_scores / jnp.sum(exp_scores, axis=-1, keepdims=True)
    probs_low = probs_vals.astype(jnp.bfloat16)
    attn_mix = jnp.einsum("hqk,khd->qhd", probs_low, heads_v, preferred_element_type=jnp.float32)
    attn_mix = attn_mix.reshape(full_len, block).astype(jnp.bfloat16)
    attn_part = jnp.dot(attn_mix, mat_out, preferred_element_type=jnp.float32)
    attn_out = lax.psum_scatter(
        attn_part.astype(jnp.bfloat16), "ctx", scatter_dimension=0, tiled=True
    )
    rows_loc = tokens_loc.astype(jnp.float32)
    resid_one = rows_loc + (attn_out.astype(jnp.float32) + bias_out)

    normed_two, ln_two_pull = jax.vjp(layer_norm, resid_one, gain_two, shift_two)
    hidden_two = lax.all_gather(normed_two.astype(jnp.bfloat16), "ctx", axis=0, tiled=True)
    up_pre = jnp.dot(hidden_two, mat_up, preferred_element_type=jnp.float32) + bias_up_own
    act_out, gelu_pull = jax.vjp(gelu_tanh, up_pre)
    act_low = act_out.astype(jnp.bfloat16)
    grad_act = times_trans(dy_all, mat_down)
    grad_up_low = gelu_pull(grad_act)[0].astype(jnp.bfloat16)
    grad_normed_part = times_trans(grad_up_low, mat_up).astype(jnp.bfloat16)
    grad_normed_two = lax.psum_scatter(grad_normed_part, "ctx", scatter_dimension=0, tiled=True)
    dy_loc = jnp.where(live_loc[:, None], grads_loc, jnp.zeros_like(grads_loc)).astype(jnp.float32)
    grad_bias_down = jnp.sum(dy_loc, axis=0)
    grad_bias_up = jnp.sum(grad_up_low.astype(jnp.float32), axis=0)
    grad_resid_ln, grad_gain_two, grad_shift_two = ln_two_pull(grad_normed_two.astype(jnp.float32))
    grad_resid = dy_loc + grad_resid_ln
    grad_attn_loc = grad_resid.astype(jnp.bfloat16)
    grad_bias_out = jnp.sum(grad_attn_loc.astype(jnp.float32), axis=0)
    grad_attn = lax.all_gather(grad_attn_loc, "ctx", axis=0, tiled=True)

    down_part = jnp.dot(act_low, mat_down, preferred_element_type=jnp.float32).astype(jnp.bfloat16)
    ffn_pack = jnp.concatenate(
        [
            outer_sum(hidden_two, grad_up_low)
            .reshape(parts, group, rows_in, hid)
            .transpose(1, 0, 2, 3)
            .reshape(group, tall, hid),
            outer_sum(act_low, dy_all).reshape(group, tall, MODEL_WIDTH),
        ],
        axis=2,
    ).astype(jnp.bfloat16)
    grad_attn, down_part, ffn_pack = lax.optimization_barrier((grad_attn, down_part, ffn_pack))
    down_out = lax.psum_scatter(down_part, "ctx", scatter_dimension=0, tiled=True)
    block_out = (resid_one + (down_out.astype(jnp.float32) + bias_down)).astype(jnp.bfloat16)[None]
    ffn_sum = lax.psum_scatter(
        ffn_pack.reshape(group * tall, -1), "fsdp", scatter_dimension=0, tiled=True
    )

    grad_mixed = times_trans(grad_attn, mat_out).astype(jnp.bfloat16)
    grad_mixed = grad_mixed.reshape(full_len, heads, HEAD_DIM)
    grad_value = jnp.einsum(
        "hqk,qhd->khd", probs_low, grad_mixed, preferred_element_type=jnp.float32
    )
    grad_probs = jnp.einsum("qhd,khd->hqk", grad_mixed, heads_v, preferred_element_type=jnp.float32)
    grad_scores = probs_vals * (
        grad_probs - jnp.sum(probs_vals * grad_probs, axis=-1, keepdims=True)
    )
    grad_scores_low = grad_scores.astype(jnp.bfloat16)
    grad_query = (
        jnp.einsum("hqk,khd->qhd", grad_scores_low, heads_k, preferred_element_type=jnp.float32)
        * score_scale
    )
    grad_key = (
        jnp.einsum("hqk,qhd->khd", grad_scores_low, heads_q, preferred_element_type=jnp.float32)
        * score_scale
    )
    grad_qkv_low = jnp.concatenate(
        [part.reshape(full_len, block) for part in (grad_query, grad_key, grad_value)], axis=1
    ).astype(jnp.bfloat16)
    grad_bias_qkv = jnp.sum(grad_qkv_low.astype(jnp.float32), axis=0)
    grad_first_part = times_trans(grad_qkv_low, mat_qkv).astype(jnp.bfloat16)
    grad_normed_one = lax.psum_scatter(grad_first_part, "ctx", scatter_dimension=0, tiled=True)
    _, ln_one_pull = jax.vjp(layer_norm, rows_loc, gain_one, shift_one)
    grad_rows_ln, grad_gain_one, grad_shift_one = ln_one_pull(grad_normed_one.astype(jnp.float32))
    tokens_grad = (grad_resid + grad_rows_ln)[None]

    def own_columns(values, count):
        wide_all = jnp.zeros((count, parts, values.size // count), jnp.float32)
        return lax.dynamic_update_slice(
            wide_all, values.reshape(count, 1, -1), (0, own, 0)
        ).reshape(-1)

    grad_vec = jnp.concatenate(
        [
            grad_gain_one,
            grad_shift_one,
            own_columns(grad_bias_qkv, 3),
            grad_bias_out,
            grad_gain_two,
            grad_shift_two,
            own_columns(grad_bias_up, 1),
            grad_bias_down,
        ]
    )
    attn_wide = wide_qkv + fold_wide
    attn_pack = jnp.concatenate(
        [
            outer_sum(hidden_one, grad_qkv_low)
            .reshape(parts, group, rows_in, wide_qkv)
            .transpose(1, 0, 2, 3)
            .reshape(group, tall, wide_qkv),
            outer_sum(attn_mix, grad_attn)
            .reshape(group, rows_out, folds, fold_wide)
            .transpose(0, 2, 1, 3)
            .reshape(group, tall, fold_wide),
        ],
        axis=2,
    )
    vec_pack = jnp.pad(
        grad_vec.reshape(parts, group, vec_len).transpose(1, 0, 2),
        ((0, 0), (0, 16 - parts), (0, attn_wide - vec_len)),
    )
    attn_pack = jnp.concatenate([attn_pack, vec_pack], axis=1).astype(jnp.bfloat16)
    attn_sum = lax.psum_scatter(
        attn_pack.reshape(group * (tall + 16), attn_wide), "fsdp", scatter_dimension=0, tiled=True
    )

    total_ffn = lax.psum(ffn_sum, "replica")
    ffn_cols = lax.all_to_all(total_ffn[:, :hid].reshape(parts, rows_in, hid), "ctx", 0, 0)
    total_up = ffn_cols.transpose(1, 0, 2).reshape(w_up.shape).astype(jnp.float32)
    total_down = total_ffn[:, hid:].astype(jnp.float32)
    total_attn = lax.psum(attn_sum, "replica")
    total_out = (
        total_attn[:tall, wide_qkv:]
        .reshape(folds, rows_out, fold_wide)
        .transpose(1, 0, 2)
        .reshape(w_attn_out.shape)
        .astype(jnp.float32)
    )
    vec_send = jnp.pad(
        total_attn[tall : tall + parts, :vec_len], ((0, 0), (0, 2 * wide_qkv - vec_len))
    ).reshape(parts, 2, wide_qkv)
    qkv_cols = lax.all_to_all(
        jnp.concatenate(
            [
                total_attn[:tall, :wide_qkv].reshape(parts, rows_in, wide_qkv),
                jnp.pad(vec_send, ((0, 0), (0, 14), (0, 0))),
            ],
            axis=1,
        ),
        "ctx",
        0,
        0,
    )
    total_qkv = (
        qkv_cols[:, :rows_in]
        .reshape(parts, rows_in, 3, block)
        .transpose(1, 2, 0, 3)
        .reshape(w_qkv.shape)
        .astype(jnp.float32)
    )
    total_vec = jnp.sum(
        qkv_cols[:, rows_in : rows_in + 2].astype(jnp.float32), axis=0
    ).reshape(-1)[:vec_len]
    new_qkv, mom_qkv, sec_qkv = adamw_update(
        w_qkv, total_qkv, momentum_qkv_weight, second_qkv, 0.05, 0.1
    )
    new_out, mom_out, sec_out = adamw_update(
        w_attn_out, total_out, momentum_attn_output, second_attn_out, 0.05, 0.1
    )
    new_up, mom_up, sec_up = adamw_update(w_up, total_up, momentum_up_weight, second_up, 0.05, 0.1)
    new_down, mom_down, sec_down = adamw_update(
        w_down, total_down, momentum_down_weight, second_down, 0.05, 0.1
    )
    new_vec, mom_vec, sec_vec = adamw_update(
        vectors, total_vec, momentum_vector_rows, second_vectors, 0.6, 0.0
    )
    return (
        block_out,
        tokens_grad,
        new_qkv,
        new_out,
        new_up,
        new_down,
        new_vec,
        mom_qkv,
        mom_out,
        mom_up,
        mom_down,
        mom_vec,
        sec_qkv,
        sec_out,
        sec_up,
        sec_down,
        sec_vec,
    )


def solution(mesh):
    placed = (
        P(("fsdp", "replica"), "ctx", None),
        P(("fsdp", "replica"), "ctx", None),
        P(("fsdp", "replica"), None),
        P(("fsdp", "replica")),
        P(("ctx", "fsdp"), None),
        P(("ctx", "fsdp"), None),
        P(("ctx", "fsdp"), None),
        P(("ctx", "fsdp"), None),
        P(("ctx", "fsdp")),
        P(("ctx", "fsdp"), None),
        P(("ctx", "fsdp"), None),
        P(("ctx", "fsdp"), None),
        P(("ctx", "fsdp"), None),
        P(("ctx", "fsdp")),
        P(("ctx", "fsdp"), None),
        P(("ctx", "fsdp"), None),
        P(("ctx", "fsdp"), None),
        P(("ctx", "fsdp"), None),
        P(("ctx", "fsdp")),
    )
    return jax.shard_map(
        shards,
        mesh=mesh,
        in_specs=placed,
        out_specs=(
            P(("fsdp", "replica"), "ctx", None),
            P(("fsdp", "replica"), "ctx", None),
            P(("ctx", "fsdp"), None),
            P(("ctx", "fsdp"), None),
            P(("ctx", "fsdp"), None),
            P(("ctx", "fsdp"), None),
            P(("ctx", "fsdp")),
            P(("ctx", "fsdp"), None),
            P(("ctx", "fsdp"), None),
            P(("ctx", "fsdp"), None),
            P(("ctx", "fsdp"), None),
            P(("ctx", "fsdp")),
            P(("ctx", "fsdp"), None),
            P(("ctx", "fsdp"), None),
            P(("ctx", "fsdp"), None),
            P(("ctx", "fsdp"), None),
            P(("ctx", "fsdp")),
        ),
        check_vma=False,
    )
```

time: 1990 us -> 554 us (0.28)
  waiting for transfers between devices: 1650 us -> 387 us
  local copies, waits for them, and re-layouts: 136 us -> 35.8 us
  blocking collectives: 80.2 us -> 0 us
  matrix products: 80.2 us -> 45 us
  other arithmetic: 23.2 us -> 44.8 us
    unnamed x11, waiting for transfers between devices: 1270 us -> 1.36 us
    all_gather x6 -> x4, waiting for transfers between devices: 345 us -> 160 us  [the longest x1 68.1 us: shards(): lax.all_gather(jnp.concatenate([pack, vec_rows], axis=0), 'fsdp', axis=0,...]
    reduce_scatter x2 -> x6, waiting for transfers between devices: 15.8 us -> 188 us  [the longest x1 56 us: shards(): lax.psum_scatter(ffn_pack.reshape(group * tall, -1), 'fsdp', scatter_dime...]
    unnamed x1 -> x0, blocking collectives: 80.2 us -> none
    unnamed x93 -> x134, local copies, waits for them, and re-layouts: 54.7 us -> 5.83 us
    reshape x9 -> x13, local copies, waits for them, and re-layouts: 51.5 us -> 4.29 us  [the longest x3 2.52 us: shards(): part.reshape(full_len, block)]
    dot_general x4, matrix products: 30.7 us -> 8.07 us  [outer_sum(): lax.dot_general(left_mat, right_mat, (((0,), (0,)), ((), ())), preferred_...]
  transfers between devices with their start and end apart: 10 -> 14, of which waited for: 9 -> 13; matrix products, arithmetic and copies ran while one was open for 5% -> 9% of each run, Pallas kernels for 0% -> 0%
where the time goes in v1:
time: 554 us; the launch traced here: 544 us
  waiting for transfers between devices  387 us (70%)
  matrix products  45 us (8%)
  other arithmetic  44.8 us (8%)
  local copies, waits for them, and re-layouts  35.8 us (6%)
  between operations  16 us (3%)
  starting transfers between devices  15.5 us (3%)
    all_gather x1, waiting for transfers between devices, shards(): lax.all_gather(jnp.concatenate([pack, vec_rows], axis=0), 'fsdp', axis=0,...  68.1 us
    all_gather x1, waiting for transfers between devices, shards(): lax.all_gather(jnp.concatenate([tokens_loc, grads_loc, vec_pad], axis=0),...  59.1 us
    reduce_scatter x1, waiting for transfers between devices, shards(): lax.psum_scatter(ffn_pack.reshape(group * tall, -1), 'fsdp', scatter_dime...  56 us
    reduce_scatter x1, waiting for transfers between devices, shards(): lax.psum_scatter(attn_pack.reshape(group * (tall + 16), attn_wide), 'fsdp...  33.7 us
    reduce_scatter x1, waiting for transfers between devices, shards(): lax.psum_scatter(down_part, 'ctx', scatter_dimension=0, tiled=True)  29.8 us
    reduce_scatter x1, waiting for transfers between devices, shards(): lax.psum_scatter(attn_part.astype(jnp.bfloat16), 'ctx', scatter_dimension...  27.1 us
    reduce_scatter x1, waiting for transfers between devices, shards(): lax.psum_scatter(grad_normed_part, 'ctx', scatter_dimension=0, tiled=True)  26.7 us
    psum x1, waiting for transfers between devices, shards(): total_attn = lax.psum(attn_sum, 'replica')  19.6 us
  transfers between devices with their start and end apart: 14, of which 13 were waited for; matrix products, arithmetic and copies ran while one was open for 9% of the time, Pallas kernels for 0%

profile of v1, /device:TPU:0, one launch (start us, length us, event | category | flops | bytes accessed | tf_op | source)
XLA Modules:
  0.0 544.3 jit_solution(10843512314927407645)
XLA Ops:
  8.0 1.9 fusion.49
  13.1 6.3 %all-to-all-start = ((bf16[4,64,1792]{2,1,0:T(8,128)(2,1)}), bf16[4,64,1792]{2,1,0:T(8,128)(2,1)S(1)}, u32[]{:S(2)}, u32[]{:S(2)}) async-start(bf16[4,64,1792]{2,1,0:T(8,128)(2,1)} %copy.104), calls=%async_computation | async-start | bytes 1835008 | tf_op jit(solution)/shard_map/all_to_all | solution.py:137
  19.6 59.1 %all-gather.11.cloned.1.call-done = bf16[1088,1024]{1,0:T(8,128)(2,1)} async-done(((bf16[272,1024]{1,0:T(8,128)(2,1)}), bf16[1088,1024]{1,0:T(8,128)(2,1)}) %all-gather.11.cloned.1.call-update) | async-done | bytes 2228240 | tf_op jit(solution)/shard_map/all_gather | solution.py:119
  79.6 2.2 fusion.21
  86.3 68.1 %all-gather.13.cloned.1.call-done = bf16[1088,3072]{1,0:T(8,128)(2,1)} async-done(((bf16[272,3072]{1,0:T(8,128)(2,1)}), bf16[1088,3072]{1,0:T(8,128)(2,1)}) %all-gather.13.cloned.1.call-update) | async-done | bytes 6684688 | tf_op jit(solution)/shard_map/all_gather | solution.py:145
  156.4 2.8 slice.143
  165.5 5.9 %fusion.90 = (f32[4,512]{1,0:T(4,128)}, f32[4,512,512]{1,2,0:T(8,128)}) fusion(f32[512,512]{0,1:T(8,128)} %subtract_convert_fusion, f32[4]{0:T(128)} %dynamic_slice.10, pred[512,512]{0,1:T(8,128)(4,1)} %fusion.36, bf16[512,4,64]{0,2,1:T(8,128)(2,1)S(1)} %bitcast.233, bf16[512,4,64]{0,2,1:T(8,128)(2,1)S(1)} %bitcast.229), kind=kOutput, calls=%fused_computation.186 | convolution fusion | flops 140509696 | bytes 6037520 | tf_op jit(solution)/shard_map/sub | solution.py:191
  171.5 3.6 convolution_convert_fusion.10
  175.1 1.4 convolution_convert_fusion.6
  176.8 27.1 %reduce-scatter.7.cloned.1.call-done = bf16[128,1024]{1,0:T(8,128)(2,1)} async-done(((bf16[512,1024]{1,0:T(8,128)(2,1)}), bf16[128,1024]{1,0:T(8,128)(2,1)}) %reduce-scatter.7.cloned.1.call-update) | async-done | bytes 262160 | tf_op jit(solution)/shard_map/reduce_scatter | solution.py:197
  206.2 1.8 add_convert_fusion.4
  208.7 2.0 slice_convert_fusion
  210.8 4.0 fusion.86
  215.5 19.3 %all-gather.7.cloned.1.call-done = bf16[512,1024]{1,0:T(8,128)(2,1)} async-done(((bf16[128,1024]{1,0:T(8,128)(2,1)}), bf16[512,1024]{1,0:T(8,128)(2,1)}) %all-gather.7.cloned.1.call-update) | async-done | bytes 1048592 | tf_op jit(solution)/shard_map/all_gather | solution.py:204
  234.8 4.1 fusion.15
  238.8 2.9 convert_reduce_fusion
  241.8 2.3 convolution_convert_fusion.5
  244.1 26.7 %reduce-scatter.9.cloned.1.call-done = bf16[128,1024]{1,0:T(8,128)(2,1)} async-done(((bf16[512,1024]{1,0:T(8,128)(2,1)}), bf16[128,1024]{1,0:T(8,128)(2,1)}) %reduce-scatter.9.cloned.1.call-update) | async-done | bytes 262160 | tf_op jit(solution)/shard_map/reduce_scatter | solution.py:211
  270.8 1.3 fusion.51
  274.6 1.3 copy.136
  275.9 2.8 convolution_convert_fusion.1
  281.7 2.6 pad_maximum_fusion
  285.4 2.5 convolution_convert_fusion.4
  287.9 13.2 %all-gather.9.cloned.1.call-done = bf16[512,1024]{1,0:T(8,128)(2,1)} async-done(((bf16[128,1024]{1,0:T(8,128)(2,1)}), bf16[512,1024]{1,0:T(8,128)(2,1)}) %all-gather.9.cloned.1.call-update) | async-done | bytes 1048592 | tf_op jit(solution)/shard_map/all_gather | solution.py:219
  301.1 1.7 convolution_convert_fusion.9
  302.8 3.5 convolution_convert_fusion.8
  306.4 3.1 multiply_reduce_fusion
  314.8 3.8 convolution_convert_fusion.3
  318.6 1.9 copy.123
  320.6 3.1 add_convert_fusion
  324.0 1.3 copy.137
  325.4 2.2 fusion.22
  328.8 1.8 convolution_convert_fusion.7
  330.6 14.8 %reduce-scatter.13.cloned.1.call-done = bf16[128,1024]{1,0:T(8,128)(2,1)} async-done(((bf16[512,1024]{1,0:T(8,128)(2,1)}), bf16[128,1024]{1,0:T(8,128)(2,1)}) %reduce-scatter.13.cloned.1.call-update) | async-done | bytes 262160 | tf_op jit(solution)/shard_map/reduce_scatter | solution.py:262
  346.6 1.3 fusion.52
  349.1 1.7 fusion.4
  352.3 33.7 %reduce-scatter.15.cloned.1.call-done = bf16[272,1024]{1,0:T(8,128)(2,1)} async-done(((bf16[1088,1024]{1,0:T(8,128)(2,1)}), bf16[272,1024]{1,0:T(8,128)(2,1)}) %reduce-scatter.15.cloned.1.call-update) | async-done | bytes 557072 | tf_op jit(solution)/shard_map/reduce_scatter | solution.py:304
  386.0 56.0 %reduce-scatter.17.cloned.1.call-done = bf16[256,2048]{1,0:T(8,128)(2,1)} async-done(((bf16[1024,2048]{1,0:T(8,128)(2,1)}), bf16[256,2048]{1,0:T(8,128)(2,1)}) %reduce-scatter.17.cloned.1.call-update) | async-done | bytes 1048592 | tf_op jit(solution)/shard_map/reduce_scatter | solution.py:235
  442.0 29.8 %reduce-scatter.11.cloned.1.call-done = bf16[128,1024]{1,0:T(8,128)(2,1)} async-done(((bf16[512,1024]{1,0:T(8,128)(2,1)}), bf16[128,1024]{1,0:T(8,128)(2,1)}) %reduce-scatter.11.cloned.1.call-update) | async-done | bytes 262160 | tf_op jit(solution)/shard_map/reduce_scatter | solution.py:233
  471.8 2.1 add_bitcast_fusion
  474.0 19.6 %all-reduce.8.cloned.1.call-done = (bf16[272,1024]{1,0:T(8,128)(2,1)}, bf16[256,2048]{1,0:T(8,128)(2,1)}) async-done(((bf16[272,1024]{1,0:T(8,128)(2,1)}, bf16[256,2048]{1,0:T(8,128)(2,1)}), (bf16[272,1024]{1,0:T(8,128)(2,1)}, bf16[256,2048]{1,0:T(8,128)(2,1)})) %all-reduce.8.cloned.1.call-update) | async-done | bytes 1605648 | tf_op jit(solution)/shard_map/psum | solution.py:312
  497.2 4.9 all-to-all-start.1
  504.4 2.3 multiply_subtract_fusion
  506.7 9.7 %all-to-all-done.1 = bf16[4,80,768]{2,1,0:T(8,128)(2,1)S(1)} async-done(((bf16[4,80,768]{2,1,0:T(8,128)(2,1)}), bf16[4,80,768]{2,1,0:T(8,128)(2,1)S(1)}, u32[]{:S(2)}, u32[]{:S(2)}) %all-to-all-start.1) | async-done | bytes 491552 | tf_op jit(solution)/shard_map/all_to_all | solution.py:323
  516.3 3.5 all-to-all-start.2
  522.0 3.1 multiply_subtract_fusion.2
  525.1 8.8 %all-to-all-done.2 = bf16[4,64,1024]{2,1,0:T(8,128)(2,1)S(1)} async-done(((bf16[4,64,1024]{2,1,0:T(8,128)(2,1)}), bf16[4,64,1024]{2,1,0:T(8,128)(2,1)S(1)}, u32[]{:S(2)}, u32[]{:S(2)}) %all-to-all-start.2) | async-done | bytes 524320 | tf_op jit(solution)/shard_map/all_to_all | solution.py:309
  535.1 2.2 multiply_subtract_fusion.1
  (255 shorter events, 47.2 us)
Async XLA Ops:
  7.2 71.5 %all-gather.11.cloned.1.call-start = ((), (), s32[]{:S(2)}) async-start(), calls=%async_computation.17 | async-start | bytes 2785280 | tf_op jit(solution)/shard_map/all_gather | solution.py:119
  12.1 7.4 %copy-start.23 = (f32[64,1024]{1,0:T(8,128)S(1)}, f32[64,1024]{1,0:T(8,128)}, u32[]{:S(2)}) copy-start(f32[64,1024]{1,0:T(8,128)} %param.24) | copy-start | bytes 786436
  12.1 7.4 %copy-start.8 = (f32[256,1024]{1,0:T(8,128)S(1)}, f32[256,1024]{1,0:T(8,128)}, u32[]{:S(2)}) copy-start(f32[256,1024]{1,0:T(8,128)} %param.26) | copy-start | bytes 3145732
  13.1 66.4 %all-to-all-start = ((bf16[4,64,1792]{2,1,0:T(8,128)(2,1)}), bf16[4,64,1792]{2,1,0:T(8,128)(2,1)S(1)}, u32[]{:S(2)}, u32[]{:S(2)}) async-start(bf16[4,64,1792]{2,1,0:T(8,128)(2,1)} %copy.104), calls=%async_computation | async-start | bytes 1835008 | tf_op jit(solution)/shard_map/all_to_all | solution.py:137
  19.5 135.0 %all-gather.13.cloned.1.call-start = ((), (), s32[]{:S(2)}) async-start(), calls=%async_computation.18 | async-start | bytes 8355840 | tf_op jit(solution)/shard_map/all_gather | solution.py:145
  81.8 122.1 %reduce-scatter.7.cloned.1.call-start = ((), (), s32[]{:S(2)}) async-start(), calls=%async_computation.9 | async-start | bytes 1310720 | tf_op jit(solution)/shard_map/reduce_scatter | solution.py:197
  163.5 8.0 %copy-start.25 = (bf16[512,256]{0,1:T(8,128)(2,1)}, bf16[512,256]{0,1:T(8,128)(2,1)S(1)}, u32[]{:S(2)}) copy-start(bf16[512,256]{0,1:T(8,128)(2,1)S(1)} %copy.111) | copy-start | bytes 786436
  164.7 6.8 %copy-start.27 = (bf16[512,256]{0,1:T(8,128)(2,1)}, bf16[512,256]{0,1:T(8,128)(2,1)S(1)}, u32[]{:S(2)}) copy-start(bf16[512,256]{0,1:T(8,128)(2,1)S(1)} %copy.110) | copy-start | bytes 786436
  175.1 32.9 %copy-start.22 = (bf16[4,64,512]{2,1,0:T(8,128)(2,1)}, bf16[4,64,512]{2,1,0:T(8,128)(2,1)S(1)}, u32[]{:S(2)}) copy-start(bf16[4,64,512]{2,1,0:T(8,128)(2,1)S(1)} %convolution_convert_fusion.10) | copy-start | bytes 786436
  175.1 28.8 %copy-start = (bf16[1,128,1024]{2,1,0:T(8,128)(2,1)S(1)}, bf16[1,128,1024]{2,1,0:T(8,128)(2,1)}, u32[]{:S(2)}) copy-start(bf16[1,128,1024]{2,1,0:T(8,128)(2,1)} %param.19) | copy-start | bytes 786436
  175.1 31.1 %copy-start.46 = (f32[1024]{0:T(1024)S(1)}, f32[1024]{0:T(1024)}, u32[]{:S(2)}) copy-start(f32[1024]{0:T(1024)} %get-tuple-element.70) | copy-start | bytes 12292
  176.6 58.2 %all-gather.7.cloned.1.call-start = ((), (), s32[]{:S(2)}) async-start(), calls=%async_computation.10 | async-start | bytes 1310720 | tf_op jit(solution)/shard_map/all_gather | solution.py:204
  208.0 62.8 %reduce-scatter.9.cloned.1.call-start = ((), (), s32[]{:S(2)}) async-start(), calls=%async_computation.11 | async-start | bytes 1310720 | tf_op jit(solution)/shard_map/reduce_scatter | solution.py:211
  215.5 23.3 %copy-start.15 = (bf16[4,4,64,1024]{3,2,1,0:T(8,128)(2,1)}, bf16[4,4,64,1024]{3,2,1,0:T(8,128)(2,1)S(1)}, u32[]{:S(2)}) copy-start(bf16[4,4,64,1024]{3,2,1,0:T(8,128)(2,1)S(1)} %copy.114) | copy-start | bytes 6291460
  234.8 4.1 copy-start.17
  234.8 4.1 copy-start.38
  241.7 29.1 %copy-start.2 = (bf16[128,1024]{1,0:T(8,128)(2,1)S(1)}, bf16[128,1024]{1,0:T(8,128)(2,1)}, u32[]{:S(2)}) copy-start(bf16[128,1024]{1,0:T(8,128)(2,1)} %reduce-scatter.7.cloned.1.call-done) | copy-start | bytes 786436
  244.0 29.4 %copy-start.14 = (bf16[1,128,1024]{2,1,0:T(8,128)(2,1)S(1)}, bf16[1,128,1024]{2,1,0:T(8,128)(2,1)}, u32[]{:S(2)}) copy-start(bf16[1,128,1024]{2,1,0:T(8,128)(2,1)} %param.20) | copy-start | bytes 786436
  244.0 30.6 %copy-start.34 = (bf16[1024,512]{0,1:T(8,128)(2,1)S(1)}, bf16[1024,512]{0,1:T(8,128)(2,1)}, u32[]{:S(2)}) copy-start(bf16[1024,512]{0,1:T(8,128)(2,1)} %get-tuple-element.83) | copy-start | bytes 3145732
  244.1 57.0 %all-gather.9.cloned.1.call-start = ((), (), s32[]{:S(2)}) async-start(), calls=%async_computation.12 | async-start | bytes 1310720 | tf_op jit(solution)/shard_map/all_gather | solution.py:219
  244.1 31.8 %copy-start.54 = (pred[128]{0:T(512)(128)(4,1)}, pred[128]{0:T(512)(128)(4,1)S(1)}, u32[]{:S(2)}) copy-start(pred[128]{0:T(512)(128)(4,1)S(1)} %add_compare_fusion.1) | copy-start | bytes 388
  273.4 5.4 copy-start.56
  274.3 71.0 %reduce-scatter.13.cloned.1.call-start = ((), (), s32[]{:S(2)}) async-start(), calls=%async_computation.14 | async-start | bytes 1310720 | tf_op jit(solution)/shard_map/reduce_scatter | solution.py:262
  281.7 3.7 copy-start.60
  285.4 17.4 %copy-start.26 = (bf16[512,256]{0,1:T(8,128)(2,1)S(1)}, bf16[512,256]{0,1:T(8,128)(2,1)}, u32[]{:S(2)}) copy-start(bf16[512,256]{0,1:T(8,128)(2,1)} %copy-done.25) | copy-start | bytes 786436
  285.4 17.4 %copy-start.28 = (bf16[512,256]{0,1:T(8,128)(2,1)S(1)}, bf16[512,256]{0,1:T(8,128)(2,1)}, u32[]{:S(2)}) copy-start(bf16[512,256]{0,1:T(8,128)(2,1)} %copy-done.27) | copy-start | bytes 786436
  285.4 17.4 %copy-start.48 = (f32[4,512]{1,0:T(4,128)S(1)}, f32[4,512]{1,0:T(4,128)}, u32[]{:S(2)}) copy-start(f32[4,512]{1,0:T(4,128)} %get-tuple-element.81) | copy-start | bytes 24580
  285.4 17.4 %copy-start.58 = (f32[4]{0:T(128)S(1)}, f32[4]{0:T(128)}, u32[]{:S(2)}) copy-start(f32[4]{0:T(128)} %dynamic_slice.10) | copy-start | bytes 52
  314.8 3.9 copy-start.3
  318.6 67.4 %reduce-scatter.15.cloned.1.call-start = ((), (), s32[]{:S(2)}) async-start(), calls=%async_computation.15 | async-start | bytes 2785280 | tf_op jit(solution)/shard_map/reduce_scatter | solution.py:304
  320.5 4.8 copy-start.29
  320.6 4.8 copy-start.30
  320.6 4.8 copy-start.31
  350.9 91.1 %reduce-scatter.17.cloned.1.call-start = ((), (), s32[]{:S(2)}) async-start(), calls=%async_computation.16 | async-start | bytes 5242880 | tf_op jit(solution)/shard_map/reduce_scatter | solution.py:235
  351.6 120.2 %copy-start.10 = (bf16[128,1024]{1,0:T(8,128)(2,1)S(1)}, bf16[128,1024]{1,0:T(8,128)(2,1)}, u32[]{:S(2)}) copy-start(bf16[128,1024]{1,0:T(8,128)(2,1)} %reduce-scatter.13.cloned.1.call-done) | copy-start | bytes 786436
  351.6 120.2 %copy-start.45 = (f32[1024]{0:T(1024)S(1)}, f32[1024]{0:T(1024)}, u32[]{:S(2)}) copy-start(f32[1024]{0:T(1024)} %get-tuple-element.69) | copy-start | bytes 12292
  351.6 120.2 %copy-start.55 = (pred[128]{0:T(512)(128)(4,1)S(1)}, pred[128]{0:T(512)(128)(4,1)}, u32[]{:S(2)}) copy-start(pred[128]{0:T(512)(128)(4,1)} %copy-done.54) | copy-start | bytes 388
  351.6 120.2 %copy-start.57 = (f32[128]{0:T(128)S(1)}, f32[128]{0:T(128)}, u32[]{:S(2)}) copy-start(f32[128]{0:T(128)} %copy-done.56) | copy-start | bytes 1540
  351.6 120.2 %reduce-scatter.11.cloned.1.call-start = ((), (), s32[]{:S(2)}) async-start(), calls=%async_computation.13 | async-start | bytes 1310720 | tf_op jit(solution)/shard_map/reduce_scatter | solution.py:233
  352.2 141.3 %all-reduce.8.cloned.1.call-start = ((), (), s32[]{:S(2)}) async-start(), calls=%async_computation.19 | async-start | bytes 3211264 | tf_op jit(solution)/shard_map/psum | solution.py:312
  493.5 8.6 %copy-start.40 = (bf16[256,2048]{1,0:T(8,128)(2,1)S(1)}, bf16[256,2048]{1,0:T(8,128)(2,1)}, u32[]{:S(2)}) copy-start(bf16[256,2048]{1,0:T(8,128)(2,1)} %get-tuple-element.31) | copy-start | bytes 3145732
  496.3 6.7 %copy-start.24 = (f32[64,1024]{1,0:T(8,128)S(1)}, f32[64,1024]{1,0:T(8,128)}, u32[]{:S(2)}) copy-start(f32[64,1024]{1,0:T(8,128)} %param.24) | copy-start | bytes 786436
  496.3 6.7 %copy-start.41 = (f32[64,1024]{1,0:T(8,128)S(1)}, f32[64,1024]{1,0:T(8,128)}, u32[]{:S(2)}) copy-start(f32[64,1024]{1,0:T(8,128)} %param.29) | copy-start | bytes 786436
  496.3 6.7 %copy-start.42 = (f32[64,1024]{1,0:T(8,128)S(1)}, f32[64,1024]{1,0:T(8,128)}, u32[]{:S(2)}) copy-start(f32[64,1024]{1,0:T(8,128)} %param.34) | copy-start | bytes 786436
  497.2 19.1 %all-to-all-start.1 = ((bf16[4,80,768]{2,1,0:T(8,128)(2,1)}), bf16[4,80,768]{2,1,0:T(8,128)(2,1)S(1)}, u32[]{:S(2)}, u32[]{:S(2)}) async-start(bf16[4,80,768]{2,1,0:T(8,128)(2,1)} %fusion.55), calls=%async_computation.6 | async-start | bytes 983040 | tf_op jit(solution)/shard_map/all_to_all | solution.py:323
  516.3 17.6 %all-to-all-start.2 = ((bf16[4,64,1024]{2,1,0:T(8,128)(2,1)}), bf16[4,64,1024]{2,1,0:T(8,128)(2,1)S(1)}, u32[]{:S(2)}, u32[]{:S(2)}) async-start(bf16[4,64,1024]{2,1,0:T(8,128)(2,1)} %bitcast.69), calls=%async_computation.8 | async-start | bytes 1048576 | tf_op jit(solution)/shard_map/all_to_all | solution.py:309
  525.1 9.0 %copy-start.7 = (f32[64,4096]{1,0:T(8,128)S(1)}, f32[64,4096]{1,0:T(8,128)}, u32[]{:S(2)}) copy-start(f32[64,4096]{1,0:T(8,128)} %param.25) | copy-start | bytes 3145732
  525.1 9.0 %copy-start.20 = (f32[64,4096]{1,0:T(8,128)S(1)}, f32[64,4096]{1,0:T(8,128)}, u32[]{:S(2)}) copy-start(f32[64,4096]{1,0:T(8,128)} %param.30) | copy-start | bytes 3145732
  (29 other events, 58.0 us)
Sparse Core Ops, SparseCore 0:
  10.2 68.4 all-gather.10
  81.9 72.4 all-gather.12
  176.7 27.1 reduce-scatter.6
  208.1 26.5 all-gather.6
  244.2 26.6 reduce-scatter.8
  274.5 26.5 all-gather.8
  318.7 26.6 reduce-scatter.12
  351.0 34.9 reduce-scatter.14
  389.2 52.6 reduce-scatter.16
  444.7 27.1 reduce-scatter.10
  474.3 19.1 all-reduce.7

commit v2 on v1

--- a/solution.py
+++ b/solution.py
@@ -1,6 +1,10 @@
+import functools
+
 import jax
 import jax.numpy as jnp
 from jax import lax
+from jax.experimental import pallas as pl
+from jax.experimental.pallas import tpu as pltpu
 from jax.sharding import PartitionSpec as P
 
 MODEL_WIDTH = 1024
@@ -8,6 +12,8 @@
 HEAD_DIM = 64
 HIDDEN_UNITS = 4096
 STEP = 10
+
+MESH = pl.DeviceIdType.MESH
 
 
 norm_eps = 1e-05
@@ -73,6 +79,217 @@
         first_hat / (jnp.sqrt(second_hat) + adam_eps) + decay_rate * weight
     )
     return (weight_new, first_new, second_new)
+
+
+def enter(group, me_f, me_r):
+    barrier = pltpu.get_barrier_semaphore()
+    for step in range(1, group):
+        pl.semaphore_signal(
+            barrier, inc=1, device_id={"fsdp": lax.rem(me_f + step, group)}, device_id_type=MESH
+        )
+    pl.semaphore_signal(barrier, inc=1, device_id={"replica": 1 - me_r}, device_id_type=MESH)
+    pl.semaphore_wait(barrier, group)
+
+
+def gather_kernel(group, kinds, *refs):
+    count = len(kinds)
+    ins, outs = refs[:count], refs[count : 2 * count]
+    local_sem, send_sem, recv_sem, pass_send, pass_recv = refs[2 * count :]
+    me_f, me_r = lax.axis_index("fsdp"), lax.axis_index("replica")
+    enter(group, me_f, me_r)
+
+    def spot(index, owner, half):
+        if kinds[index]:
+            return outs[index].at[half, owner]
+        return outs[index].at[owner, half]
+
+    halves, waits = [], []
+    for index in range(count):
+        size = ins[index].shape[0] // 2
+        halves.append(pl.ds(me_r * size, size))
+    for index in range(count):
+        for step in range(1, group):
+            copy = pltpu.make_async_remote_copy(
+                src_ref=ins[index].at[halves[index]],
+                dst_ref=spot(index, me_f, halves[index]),
+                send_sem=send_sem.at[index, step - 1],
+                recv_sem=recv_sem.at[index, step - 1],
+                device_id={"fsdp": lax.rem(me_f + step, group)},
+                device_id_type=MESH,
+            )
+            copy.start()
+            waits.append((copy, index, step))
+    own = []
+    for index in range(count):
+        whole = pl.ds(0, ins[index].shape[0])
+        copy = pltpu.make_async_copy(ins[index], spot(index, me_f, whole), local_sem.at[index])
+        copy.start()
+        own.append(copy)
+    passed = []
+    for copy, index, step in waits:
+        copy.wait_recv()
+        sender = lax.rem(me_f + group - step, group)
+        part = spot(index, sender, halves[index])
+        onward = pltpu.make_async_remote_copy(
+            src_ref=part,
+            dst_ref=part,
+            send_sem=pass_send.at[index, step - 1],
+            recv_sem=pass_recv.at[index, step - 1],
+            device_id={"replica": 1 - me_r},
+            device_id_type=MESH,
+        )
+        onward.start()
+        passed.append(onward)
+    for copy, _, _ in waits:
+        copy.wait_send()
+    for copy in own:
+        copy.wait()
+    for copy in passed:
+        copy.wait()
+
+
+def gather_over_group(arrays, kinds, group):
+    shapes = [
+        (item.shape[0], group) + item.shape[1:] if kind else (group,) + item.shape
+        for item, kind in zip(arrays, kinds)
+    ]
+    count = len(arrays)
+    return pl.pallas_call(
+        functools.partial(gather_kernel, group, kinds),
+        out_shape=[
+            jax.ShapeDtypeStruct(shape, item.dtype) for shape, item in zip(shapes, arrays)
+        ],
+        in_specs=[pl.BlockSpec(memory_space=pl.ANY)] * count,
+        out_specs=[pl.BlockSpec(memory_space=pl.ANY)] * count,
+        scratch_shapes=[pltpu.SemaphoreType.DMA((count,))]
+        + [pltpu.SemaphoreType.DMA((count, group - 1))] * 4,
+        compiler_params=pltpu.CompilerParams(collective_id=0, has_side_effects=True),
+        cost_estimate=pl.CostEstimate(flops=0, bytes_accessed=120_000_000, transcendentals=0),
+    )(*arrays)
+
+
+def reduce_kernel(group, kinds, *refs):
+    count = len(kinds)
+    ins, outs = refs[:count], refs[count : 2 * count]
+    firsts, seconds = refs[2 * count : 3 * count], refs[3 * count : 4 * count]
+    core_send, core_recv, send_sem, recv_sem, pass_send, pass_recv = refs[4 * count :]
+    me_f, me_r = lax.axis_index("fsdp"), lax.axis_index("replica")
+    enter(group, me_f, me_r)
+    sizes = [out.shape[0] // 2 for out in outs]
+
+    def core_copy(source, target, sends, recvs, index):
+        return pltpu.make_async_remote_copy(
+            src_ref=source,
+            dst_ref=target,
+            send_sem=sends.at[index],
+            recv_sem=recvs.at[index],
+            device_id={"replica": 1 - me_r},
+            device_id_type=MESH,
+        )
+
+    def at(ref, index, half, owner):
+        return ref.at[half, owner] if kinds[index] else ref.at[owner, half]
+
+    every = pl.ds(0, group)
+    first_copies = []
+    for index in range(count):
+        other = pl.ds((1 - me_r) * sizes[index], sizes[index])
+        copy = core_copy(
+            at(ins[index], index, other, every), firsts[index], core_send, core_recv, index
+        )
+        copy.start()
+        first_copies.append(copy)
+    peer_copies = []
+    for index in range(count):
+        first_copies[index].wait_recv()
+        for step in list(range(1, group)) + [0]:
+            owner = lax.rem(me_f + step, group)
+
+            def add(place, carry, index=index, owner=owner):
+                here = at(firsts[index], index, place, owner)
+                mine = at(ins[index], index, me_r * sizes[index] + place, owner)
+                here[...] = (
+                    here[...].astype(jnp.float32) + mine[...].astype(jnp.float32)
+                ).astype(here.dtype)
+                return carry
+
+            lax.fori_loop(0, sizes[index], add, 0)
+            if step:
+                copy = pltpu.make_async_remote_copy(
+                    src_ref=at(firsts[index], index, pl.ds(0, sizes[index]), owner),
+                    dst_ref=seconds[index].at[step - 1],
+                    send_sem=send_sem.at[index, step - 1],
+                    recv_sem=recv_sem.at[index, step - 1],
+                    device_id={"fsdp": owner},
+                    device_id_type=MESH,
+                )
+                copy.start()
+                peer_copies.append(copy)
+    last_copies = []
+    for index in range(count):
+        for step in range(1, group):
+            peer_copies[index * (group - 1) + step - 1].wait_recv()
+
+        def total(place, carry, index=index):
+            value = at(firsts[index], index, place, me_f)[...].astype(jnp.float32)
+            for step in range(1, group):
+                value += seconds[index][step - 1, place].astype(jnp.float32)
+            outs[index][me_r * sizes[index] + place] = value.astype(outs[index].dtype)
+            return carry
+
+        lax.fori_loop(0, sizes[index], total, 0)
+        part = outs[index].at[pl.ds(me_r * sizes[index], sizes[index])]
+        copy = core_copy(part, part, pass_send, pass_recv, index)
+        copy.start()
+        last_copies.append(copy)
+    for copy in first_copies + peer_copies:
+        copy.wait_send()
+    for copy in last_copies:
+        copy.wait()
+
+
+def reduce_over_group(arrays, kinds, group, name):
+    count = len(arrays)
+    outs, firsts, seconds = [], [], []
+    for item, kind in zip(arrays, kinds):
+        lead = item.shape[0] if kind else item.shape[1]
+        rest = item.shape[2:]
+        outs.append((lead,) + rest)
+        half = lead // 2
+        firsts.append(((half, group) if kind else (group, half)) + rest)
+        seconds.append((group - 1, half) + rest)
+    return pl.pallas_call(
+        functools.partial(reduce_kernel, group, kinds),
+        out_shape=[
+            jax.ShapeDtypeStruct(shape, item.dtype) for shape, item in zip(outs, arrays)
+        ],
+        in_specs=[pl.BlockSpec(memory_space=pltpu.VMEM)] * count,
+        out_specs=[pl.BlockSpec(memory_space=pltpu.VMEM)] * count,
+        scratch_shapes=[
+            pltpu.VMEM(shape, item.dtype) for shape, item in zip(firsts + seconds, arrays + arrays)
+        ]
+        + [pltpu.SemaphoreType.DMA((count,))] * 2
+        + [pltpu.SemaphoreType.DMA((count, group - 1))] * 2
+        + [pltpu.SemaphoreType.DMA((count,))] * 2,
+        compiler_params=pltpu.CompilerParams(
+            collective_id=name, has_side_effects=True, vmem_limit_bytes=24 * 1024 * 1024
+        ),
+        cost_estimate=pl.CostEstimate(flops=0, bytes_accessed=100_000_000, transcendentals=0),
+    )(*arrays)
+
+
+def plain_gather(arrays, kinds, group):
+    return [
+        lax.all_gather(item, "fsdp", axis=1 if kind else 0, tiled=False)
+        for item, kind in zip(arrays, kinds)
+    ]
+
+
+def plain_reduce(arrays, kinds, group, name):
+    return [
+        lax.psum(lax.psum_scatter(item, "fsdp", scatter_dimension=1 if kind else 0), "replica")
+        for item, kind in zip(arrays, kinds)
+    ]
 
 
 def shards(
@@ -102,9 +319,9 @@
     hid = HIDDEN_UNITS // parts
     heads = HEADS // parts
     rows_in, rows_out, vec_len = w_qkv.shape[0], w_attn_out.shape[0], vectors.shape[0]
-    tall = parts * rows_in
-    folds = tall // rows_out
-    fold_wide = MODEL_WIDTH // folds
+    paired = lax.axis_size("replica") == 2
+    gather_all = gather_over_group if paired else plain_gather
+    reduce_all = reduce_over_group if paired else plain_reduce
     wide_qkv = 3 * block
     tokens_loc, grads_loc = tokens[0], output_gradient[0]
     length = tokens_loc.shape[0]
@@ -115,15 +332,12 @@
     place_loc = own * length + jnp.arange(length, dtype=jnp.int32)
     live_loc = place_loc < row_fill[0]
 
-    vec_pad = jnp.pad(vectors.astype(jnp.bfloat16)[None, :], ((0, 15), (0, MODEL_WIDTH - vec_len)))
-    seq_pack = lax.all_gather(
-        jnp.concatenate([tokens_loc, grads_loc, vec_pad], axis=0), "ctx", axis=0, tiled=False
-    )
-    rows_all = seq_pack[:, :length].reshape(full_len, MODEL_WIDTH).astype(jnp.float32)
-    dy_all = seq_pack[:, length : 2 * length].reshape(full_len, MODEL_WIDTH)
+    rows_all = lax.all_gather(tokens_loc, "ctx", axis=0, tiled=True).astype(jnp.float32)
+    dy_all = lax.all_gather(grads_loc, "ctx", axis=0, tiled=True)
     dy_all = jnp.where(live_all[:, None], dy_all, jnp.zeros_like(dy_all))
-    vec_ctx = seq_pack[:, 2 * length]
-
+
+    vec_tile = jnp.pad(vectors.astype(jnp.bfloat16), (0, 2048 - vec_len)).reshape(16, 128)
+    vec_tile = jnp.pad(vec_tile, ((0, 0), (0, wide_qkv + hid - 128)))
     send = jnp.concatenate(
         [
             w_qkv.astype(jnp.bfloat16)
@@ -134,34 +348,26 @@
         ],
         axis=2,
     )
-    cols = lax.all_to_all(send, "ctx", 0, 0).reshape(tall, wide_qkv + hid)
-    low_out = w_attn_out.astype(jnp.bfloat16)
-    out_fold = jnp.concatenate(
-        [low_out[:, i * fold_wide : (i + 1) * fold_wide] for i in range(folds)], axis=0
-    )
-    wide = wide_qkv + hid + MODEL_WIDTH + fold_wide
-    pack = jnp.concatenate([cols, w_down.astype(jnp.bfloat16), out_fold], axis=1)
-    vec_rows = jnp.pad(vec_ctx, ((0, 16 - parts), (0, wide - MODEL_WIDTH)))
-    full = lax.all_gather(jnp.concatenate([pack, vec_rows], axis=0), "fsdp", axis=0, tiled=False)
-    mats = full[:, :tall]
-
-    def columns_whole(part):
-        return (
-            part.reshape(group, parts, rows_in, -1)
-            .transpose(1, 0, 2, 3)
-            .reshape(parts * group * rows_in, -1)
-        )
-
-    mat_qkv = columns_whole(mats[:, :, :wide_qkv])
-    mat_up = columns_whole(mats[:, :, wide_qkv : wide_qkv + hid])
-    mat_down = mats[:, :, wide_qkv + hid : wide_qkv + hid + MODEL_WIDTH].reshape(hid, MODEL_WIDTH)
-    mat_out = (
-        mats[:, :, wide_qkv + hid + MODEL_WIDTH :]
-        .reshape(group, folds, rows_out, fold_wide)
-        .transpose(0, 2, 1, 3)
-        .reshape(block, MODEL_WIDTH)
-    )
-    vec_full = full[:, tall : tall + parts, :vec_len].transpose(1, 0, 2).reshape(-1)
+    send = jnp.concatenate(
+        [send, jnp.broadcast_to(vec_tile[None], (parts,) + vec_tile.shape)], axis=1
+    )
+    cols = lax.all_to_all(send, "ctx", 0, 0)
+    mat_qkv, mat_out, mat_up, mat_down, vec_full = gather_all(
+        [
+            cols[:, :rows_in, :wide_qkv],
+            w_attn_out.astype(jnp.bfloat16).reshape(2, rows_out // 2, MODEL_WIDTH),
+            cols[:, :rows_in, wide_qkv:],
+            w_down.astype(jnp.bfloat16).reshape(parts, -1, MODEL_WIDTH),
+            cols[:, rows_in:, :128],
+        ],
+        (True, False, True, False, True),
+        group,
+    )
+    mat_qkv = mat_qkv.reshape(MODEL_WIDTH, wide_qkv)
+    mat_up = mat_up.reshape(MODEL_WIDTH, hid)
+    mat_down = mat_down.reshape(hid, MODEL_WIDTH)
+    mat_out = mat_out.reshape(block, MODEL_WIDTH)
+    vec_full = vec_full.reshape(parts * group, 2048)[:, :vec_len].reshape(-1)
     gain_one, shift_one, bias_qkv, bias_out, gain_two, shift_two, bias_up, bias_down = split_small(
         vec_full.astype(jnp.float32)
     )
@@ -219,21 +425,21 @@
     grad_attn = lax.all_gather(grad_attn_loc, "ctx", axis=0, tiled=True)
 
     down_part = jnp.dot(act_low, mat_down, preferred_element_type=jnp.float32).astype(jnp.bfloat16)
-    ffn_pack = jnp.concatenate(
+    grad_attn, down_part = lax.optimization_barrier((grad_attn, down_part))
+    down_out = lax.psum_scatter(down_part, "ctx", scatter_dimension=0, tiled=True)
+    block_out = (resid_one + (down_out.astype(jnp.float32) + bias_down)).astype(jnp.bfloat16)[None]
+    sum_up, sum_down = reduce_all(
         [
             outer_sum(hidden_two, grad_up_low)
-            .reshape(parts, group, rows_in, hid)
-            .transpose(1, 0, 2, 3)
-            .reshape(group, tall, hid),
-            outer_sum(act_low, dy_all).reshape(group, tall, MODEL_WIDTH),
+            .astype(jnp.bfloat16)
+            .reshape(parts, group, rows_in, hid),
+            outer_sum(act_low, dy_all)
+            .astype(jnp.bfloat16)
+            .reshape(group, parts, -1, MODEL_WIDTH),
         ],
-        axis=2,
-    ).astype(jnp.bfloat16)
-    grad_attn, down_part, ffn_pack = lax.optimization_barrier((grad_attn, down_part, ffn_pack))
-    down_out = lax.psum_scatter(down_part, "ctx", scatter_dimension=0, tiled=True)
-    block_out = (resid_one + (down_out.astype(jnp.float32) + bias_down)).astype(jnp.bfloat16)[None]
-    ffn_sum = lax.psum_scatter(
-        ffn_pack.reshape(group * tall, -1), "fsdp", scatter_dimension=0, tiled=True
+        (True, False),
+        group,
+        1,
     )
 
     grad_mixed = times_trans(grad_attn, mat_out).astype(jnp.bfloat16)
@@ -282,51 +488,31 @@
             grad_bias_down,
         ]
     )
-    attn_wide = wide_qkv + fold_wide
-    attn_pack = jnp.concatenate(
+    vec_pack = jnp.pad(
+        grad_vec.reshape(parts, group, vec_len), ((0, 0), (0, 0), (0, 2048 - vec_len))
+    ).reshape(parts, group, 16, 128)
+    sum_qkv, sum_out, sum_vec = reduce_all(
         [
             outer_sum(hidden_one, grad_qkv_low)
-            .reshape(parts, group, rows_in, wide_qkv)
-            .transpose(1, 0, 2, 3)
-            .reshape(group, tall, wide_qkv),
+            .astype(jnp.bfloat16)
+            .reshape(parts, group, rows_in, wide_qkv),
             outer_sum(attn_mix, grad_attn)
-            .reshape(group, rows_out, folds, fold_wide)
-            .transpose(0, 2, 1, 3)
-            .reshape(group, tall, fold_wide),
+            .astype(jnp.bfloat16)
+            .reshape(group, 2, rows_out // 2, MODEL_WIDTH),
+            vec_pack.astype(jnp.bfloat16),
         ],
-        axis=2,
-    )
-    vec_pack = jnp.pad(
-        grad_vec.reshape(parts, group, vec_len).transpose(1, 0, 2),
-        ((0, 0), (0, 16 - parts), (0, attn_wide - vec_len)),
-    )
-    attn_pack = jnp.concatenate([attn_pack, vec_pack], axis=1).astype(jnp.bfloat16)
-    attn_sum = lax.psum_scatter(
-        attn_pack.reshape(group * (tall + 16), attn_wide), "fsdp", scatter_dimension=0, tiled=True
-    )
-
-    total_ffn = lax.psum(ffn_sum, "replica")
-    ffn_cols = lax.all_to_all(total_ffn[:, :hid].reshape(parts, rows_in, hid), "ctx", 0, 0)
+        (True, False, True),
+        group,
+        2,
+    )
+
+    ffn_cols = lax.all_to_all(sum_up, "ctx", 0, 0)
     total_up = ffn_cols.transpose(1, 0, 2).reshape(w_up.shape).astype(jnp.float32)
-    total_down = total_ffn[:, hid:].astype(jnp.float32)
-    total_attn = lax.psum(attn_sum, "replica")
-    total_out = (
-        total_attn[:tall, wide_qkv:]
-        .reshape(folds, rows_out, fold_wide)
-        .transpose(1, 0, 2)
-        .reshape(w_attn_out.shape)
-        .astype(jnp.float32)
-    )
-    vec_send = jnp.pad(
-        total_attn[tall : tall + parts, :vec_len], ((0, 0), (0, 2 * wide_qkv - vec_len))
-    ).reshape(parts, 2, wide_qkv)
+    total_down = sum_down.reshape(w_down.shape).astype(jnp.float32)
+    total_out = sum_out.reshape(w_attn_out.shape).astype(jnp.float32)
     qkv_cols = lax.all_to_all(
         jnp.concatenate(
-            [
-                total_attn[:tall, :wide_qkv].reshape(parts, rows_in, wide_qkv),
-                jnp.pad(vec_send, ((0, 0), (0, 14), (0, 0))),
-            ],
-            axis=1,
+            [sum_qkv, jnp.pad(sum_vec, ((0, 0), (0, 0), (0, wide_qkv - 128)))], axis=1
         ),
         "ctx",
         0,
@@ -339,9 +525,9 @@
         .reshape(w_qkv.shape)
         .astype(jnp.float32)
     )
-    total_vec = jnp.sum(
-        qkv_cols[:, rows_in : rows_in + 2].astype(jnp.float32), axis=0
-    ).reshape(-1)[:vec_len]
+    total_vec = jnp.sum(qkv_cols[:, rows_in:, :128].astype(jnp.float32), axis=0).reshape(-1)[
+        :vec_len
+    ]
     new_qkv, mom_qkv, sec_qkv = adamw_update(
         w_qkv, total_qkv, momentum_qkv_weight, second_qkv, 0.05, 0.1
     )

time: 554 us -> 405 us (0.73); the launches traced: 544 us -> 403 us
  waiting for transfers between devices: 387 us -> 168 us
  Pallas kernels: 0 us -> 102 us
  local copies, waits for them, and re-layouts: 35.8 us -> 14.9 us
  other arithmetic: 44.8 us -> 37.7 us
  matrix products: 45 us -> 51.9 us
    pallas_call x0 -> x3, Pallas kernels: none -> 102 us  [the longest x1 52.3 us: gather_over_group(): pl.pallas_call(functools.partial(gather_kernel, group, kinds), out_shape=...]
    reduce_scatter x2 -> x0, waiting for transfers between devices: 89.7 us -> none  [the longest x1 56 us: shards(): lax.psum_scatter(ffn_pack.reshape(group * tall, -1), 'fsdp', scatter_dime...]
    all_gather x2, waiting for transfers between devices: 127 us -> 63.6 us  [the longest x1 39.3 us: shards(): lax.all_gather(tokens_loc, 'ctx', axis=0, tiled=True).astype(jnp.float32)]
    reduce_scatter x1, waiting for transfers between devices: 29.8 us -> 0.01 us  [shards(): lax.psum_scatter(down_part, 'ctx', scatter_dimension=0, tiled=True)]
    psum x1 -> x0, waiting for transfers between devices: 19.6 us -> none  [shards(): total_attn = lax.psum(attn_sum, 'replica')]
    all_gather x1, waiting for transfers between devices: 13.2 us -> 0.01 us  [shards(): grad_attn = lax.all_gather(grad_attn_loc, 'ctx', axis=0, tiled=True)]
    all_to_all x3, waiting for transfers between devices: 18.4 us -> 10.3 us  [the longest x1 10.3 us: shards(): lax.all_to_all(jnp.concatenate([sum_qkv, jnp.pad(sum_vec, ((0, 0), (0, 0)...]
    concatenate x6 -> x2, other arithmetic: 9.61 us -> 1.9 us  [the longest x1 1.09 us: shards(): jnp.concatenate([send, jnp.broadcast_to(vec_tile[None], (parts,) + vec_ti...]
  transfers between devices with their start and end apart: 14 -> 11, of which waited for: 13 -> 7; matrix products, arithmetic and copies ran while one was open for 9% -> 15% of each run, Pallas kernels for 0% -> 12%
where the time goes in v2:
time: 405 us; the launch traced here: 403 us
  waiting for transfers between devices  168 us (41%)
  Pallas kernels  102 us (25%)
  matrix products  51.9 us (13%)
  other arithmetic  37.7 us (9%)
  between operations  15.5 us (4%)
  local copies, waits for them, and re-layouts  14.9 us (4%)
  starting transfers between devices  14.1 us (3%)
    pallas_call x1, Pallas kernels, gather_over_group(): pl.pallas_call(functools.partial(gather_kernel, group, kinds), out_shape=...  52.3 us
    pallas_call x2, Pallas kernels, reduce_over_group(): pl.pallas_call(functools.partial(reduce_kernel, group, kinds), out_shape=...  49.5 us
    all_gather x1, waiting for transfers between devices, shards(): lax.all_gather(tokens_loc, 'ctx', axis=0, tiled=True).astype(jnp.float32)  39.3 us
    reduce_scatter x1, waiting for transfers between devices, shards(): lax.psum_scatter(grad_normed_part, 'ctx', scatter_dimension=0, tiled=True)  26.7 us
    all_gather x1, waiting for transfers between devices, shards(): lax.all_gather(normed_two.astype(jnp.bfloat16), 'ctx', axis=0, tiled=True)  25.2 us
    reduce_scatter x1, waiting for transfers between devices, shards(): lax.psum_scatter(attn_part.astype(jnp.bfloat16), 'ctx', scatter_dimension...  25.1 us
    all_gather x1, waiting for transfers between devices, shards(): dy_all = lax.all_gather(grads_loc, 'ctx', axis=0, tiled=True)  24.3 us
    reduce_scatter x1, waiting for transfers between devices, shards(): lax.psum_scatter(grad_first_part, 'ctx', scatter_dimension=0, tiled=True)  15.3 us
  transfers between devices with their start and end apart: 11, of which 7 were waited for; matrix products, arithmetic and copies ran while one was open for 15% of the time, Pallas kernels for 12%

profile of v2, /device:TPU:0, one launch (start us, length us, event | category | flops | bytes accessed | tf_op | source)
XLA Modules:
  0.0 403.4 jit_solution(10505804949169503890)
XLA Ops:
  8.6 1.2 convert_element_type.177
  12.0 6.4 %all-to-all-start = ((bf16[4,80,1792]{2,1,0:T(8,128)(2,1)}), bf16[4,80,1792]{2,1,0:T(8,128)(2,1)}, u32[]{:S(2)}, u32[]{:S(2)}) async-start(bf16[4,80,1792]{2,1,0:T(8,128)(2,1)} %pad_maximum_fusion), calls=%async_computation | async-start | bytes 2293760 | tf_op jit(solution)/shard_map/all_to_all | solution.py:354
  21.5 39.3 %all-gather.11.cloned.1.call-done = bf16[1,512,1024]{2,1,0:T(8,128)(2,1)} async-done(((bf16[1,128,1024]{2,1,0:T(8,128)(2,1)}), bf16[1,512,1024]{2,1,0:T(8,128)(2,1)}) %all-gather.11.cloned.1.call-update) | async-done | bytes 1048592 | tf_op jit(solution)/shard_map/all_gather | solution.py:335
  60.7 1.4 convert_reduce_fusion
  62.2 1.6 fusion.5
  63.8 1.4 slice.79.refs_4_
  65.3 1.8 slice.77.refs_0_
  67.0 1.9 slice.78.refs_2_
  68.9 52.3 %shard_map.314 = (bf16[4,4,64,768]{3,2,1,0:T(8,128)(2,1)}, bf16[4,2,32,1024]{3,2,1,0:T(8,128)(2,1)}, bf16[4,4,64,1024]{3,2,1,0:T(8,128)(2,1)}, bf16[4,4,64,1024]{3,2,1,0:T(8,128)(2,1)}, bf16[4,4,16,128]{3,2,1,0:T(8,128)(2,1)}) custom-call(bf16[4,64,768]{2,1,0:T(8,128)(2,1)} %slice.77.refs_0_, bf16[2,32,1024]{2,1,0:T(8,128)(2,1)} %bitcast.217, ...), custom_call_target="tpu_custom_call" | custom-call | bytes 120000000 | tf_op jit(solution)/shard_map/pallas_call | solution.py:157
  122.4 2.5 add_convert_fusion
  126.3 4.0 fusion.78
  130.3 3.2 convolution_convert_fusion.10
  133.5 2.5 convolution_convert_fusion.6
  136.1 25.1 %reduce-scatter.5.cloned.1.call-done = bf16[128,1024]{1,0:T(8,128)(2,1)} async-done(((bf16[512,1024]{1,0:T(8,128)(2,1)}), bf16[128,1024]{1,0:T(8,128)(2,1)}) %reduce-scatter.5.cloned.1.call-update) | async-done | bytes 262160 | tf_op jit(solution)/shard_map/reduce_scatter | solution.py:403
  161.3 1.1 fusion.49
  162.4 1.2 multiply_reduce_fusion.1
  163.5 1.8 add_convert_fusion.2
  166.9 25.2 %all-gather.7.cloned.1.call-done = bf16[512,1024]{1,0:T(8,128)(2,1)} async-done(((bf16[128,1024]{1,0:T(8,128)(2,1)}), bf16[512,1024]{1,0:T(8,128)(2,1)}) %all-gather.7.cloned.1.call-update) | async-done | bytes 1048592 | tf_op jit(solution)/shard_map/all_gather | solution.py:410
  192.1 4.6 %fusion.79 = f32[512,1024]{1,0:T(8,128)} fusion(bf16[512,1024]{1,0:T(8,128)(2,1)} %all-gather.7.cloned.1.call-done, bf16[1024,1024]{1,0:T(8,128)(2,1)} %bitcast.233), kind=kOutput, calls=%fused_computation.165 | convolution fusion | flops 1073741824 | bytes 5242880 | tf_op jit(solution)/shard_map/dot_general | solution.py:411
  196.7 24.3 %all-gather.13.cloned.1.call-done = bf16[1,512,1024]{2,1,0:T(8,128)(2,1)} async-done(((bf16[1,128,1024]{2,1,0:T(8,128)(2,1)}), bf16[1,512,1024]{2,1,0:T(8,128)(2,1)}) %all-gather.13.cloned.1.call-update) | async-done | bytes 1048592 | tf_op jit(solution)/shard_map/all_gather | solution.py:336
  221.1 5.5 %convert_reduce_fusion.1 = (f32[1024]{0:T(1024)S(1)}, bf16[512,1024]{1,0:T(8,128)(2,1)S(1)}) fusion(bf16[1024,1024]{1,0:T(8,128)(2,1)} %bitcast.231, bf16[1,512,1024]{2,1,0:T(8,128)(2,1)} %all-gather.13.cloned.1.call-done, pred[512]{0:T(512)(128)(4,1)S(1)} %iota_compare_fusion.2, f32[512,1024]{1,0:T(8,128)} %fusion.79, f32[1024]{0:T(1024)S(1)} %dynamic_slice.11), kind=kOutput, calls=%fused_computation.25 | convolution fusion | flops 1088420864 | bytes 6300160 | tf_op jit(solution)/shard_map/dot_general | solution.py:68
  227.6 2.3 convolution_convert_fusion.5
  229.9 26.7 %reduce-scatter.7.cloned.1.call-done = bf16[128,1024]{1,0:T(8,128)(2,1)} async-done(((bf16[512,1024]{1,0:T(8,128)(2,1)}), bf16[128,1024]{1,0:T(8,128)(2,1)}) %reduce-scatter.7.cloned.1.call-update) | async-done | bytes 262160 | tf_op jit(solution)/shard_map/reduce_scatter | solution.py:417
  256.6 1.3 fusion.42
  257.9 1.3 fusion.74
  260.3 3.0 convolution_convert_fusion.1
  263.3 1.7 convolution_convert_fusion
  265.0 30.6 %shard_map.316 = (bf16[4,64,1024]{2,1,0:T(8,128)(2,1)}, bf16[4,64,1024]{2,1,0:T(8,128)(2,1)S(1)}) custom-call(bf16[4,4,64,1024]{3,2,1,0:T(8,128)(2,1)S(1)} %bitcast.189, bf16[4,4,64,1024]{3,2,1,0:T(8,128)(2,1)S(1)} %bitcast.190), custom_call_target="tpu_custom_call" | custom-call | bytes 100000000 | tf_op jit(solution)/shard_map/pallas_call | solution.py:261
  295.6 3.5 all-to-all-start.2
  299.3 4.7 %convolution_convert_fusion.4 = bf16[512,1024]{1,0:T(8,128)(2,1)} fusion(bf16[1024,1024]{1,0:T(8,128)(2,1)} %bitcast.232, f32[512,1024]{1,0:T(8,128)} %fusion.79, f32[1024]{0:T(1024)S(1)} %dynamic_slice.11), kind=kOutput, calls=%fused_computation.43 | convolution fusion | flops 1079508992 | bytes 5246976 | tf_op jit(solution)/shard_map/dot_general | solution.py:427
  304.1 2.5 convolution_convert_fusion.9
  306.6 4.5 %convolution_convert_fusion.8 = bf16[4,64,512]{2,1,0:T(8,128)(2,1)} fusion(bf16[512,4,64]{0,2,1:T(8,128)(2,1)} %bitcast.237, f32[4,512]{1,0:T(4,128)S(1)} %get-tuple-element.82, f32[512,512]{0,1:T(8,128)} %subtract_convert_fusion, f32[4]{0:T(128)S(1)} %dynamic_slice.10, pred[512,512]{0,1:T(8,128)(4,1)} %copy-done.26, bf16[512,4,64]{0,2,1:T(8,128)(2,1)} %bitcast.213, ...), kind=kOutput, calls=%fused_computation.49 | convolution fusion | flops 275909120 | bytes 2367504 | tf_op jit(solution)/shard_map/hqk,qhd->khd/dot_general | solution.py:447
  311.1 3.3 multiply_reduce_fusion
  314.7 1.2 multiply_convert_fusion
  318.0 2.0 convolution_convert_fusion.3
  320.2 4.2 %multiply_subtract_fusion = (f32[256,1024]{1,0:T(8,128)}, f32[256,1024]{1,0:T(8,128)}, f32[256,1024]{1,0:T(8,128)}) fusion(f32[256,1024]{1,0:T(8,128)} %param.26, bf16[4,64,1024]{2,1,0:T(8,128)(2,1)S(1)} %get-tuple-element.40, f32[256,1024]{1,0:T(8,128)} %param.31, f32[256,1024]{1,0:T(8,128)} %param.36), kind=kLoop, calls=%fused_computation.61 | loop fusion | flops 4194304 | bytes 6815744 | tf_op jit(solution)/shard_map/sub | solution.py:78
  325.9 2.2 multiply_subtract_fusion.1
  328.7 1.7 convolution_convert_fusion.7
  330.4 2.7 convolution_convert_fusion.2
  333.1 15.3 %reduce-scatter.11.cloned.1.call-done = bf16[128,1024]{1,0:T(8,128)(2,1)} async-done(((bf16[512,1024]{1,0:T(8,128)(2,1)}), bf16[128,1024]{1,0:T(8,128)(2,1)}) %reduce-scatter.11.cloned.1.call-update) | async-done | bytes 262160 | tf_op jit(solution)/shard_map/reduce_scatter | solution.py:468
  349.4 1.2 fusion.44
  350.6 1.3 fusion.43
  352.2 18.9 %shard_map.315 = (bf16[4,64,768]{2,1,0:T(8,128)(2,1)S(1)}, bf16[2,32,1024]{2,1,0:T(8,128)(2,1)S(1)}, bf16[4,16,128]{2,1,0:T(8,128)(2,1)S(1)}) custom-call(bf16[4,4,64,768]{3,2,1,0:T(8,128)(2,1)S(1)} %bitcast.192, bf16[4,2,32,1024]{3,2,1,0:T(8,128)(2,1)S(1)} %bitcast.191, bf16[4,4,16,128]{3,2,1,0:T(8,128)(2,1)S(1)} %convert_element_type.213.refs_2_), custom_call_target="tpu_custom_call" | custom-call | bytes 100000000 | tf_op jit(solution)/shard_map/pallas_call | solution.py:261
  371.9 3.5 all-to-all-start.1
  375.4 2.1 multiply_subtract_fusion.3
  377.5 2.1 add_bitcast_fusion
  379.7 10.3 %all-to-all-done.1 = bf16[4,80,768]{2,1,0:T(8,128)(2,1)S(1)} async-done(((bf16[4,80,768]{2,1,0:T(8,128)(2,1)}), bf16[4,80,768]{2,1,0:T(8,128)(2,1)S(1)}, u32[]{:S(2)}, u32[]{:S(2)}) %all-to-all-start.1) | async-done | bytes 491552 | tf_op jit(solution)/shard_map/all_to_all | solution.py:513
  393.5 3.1 multiply_subtract_fusion.2
  (168 shorter events, 22.4 us)
Async XLA Ops:
  7.2 3.6 copy-start.3
  7.2 53.5 %all-gather.11.cloned.1.call-start = ((), (), s32[]{:S(2)}) async-start(), calls=%async_computation.13 | async-start | bytes 1310720 | tf_op jit(solution)/shard_map/all_gather | solution.py:335
  10.9 7.6 %copy-start.23 = (f32[64,1024]{1,0:T(8,128)S(1)}, f32[64,1024]{1,0:T(8,128)}, u32[]{:S(2)}) copy-start(f32[64,1024]{1,0:T(8,128)} %param.24) | copy-start | bytes 786436
  10.9 8.2 %copy-start.5 = (f32[256,1024]{1,0:T(8,128)S(1)}, f32[256,1024]{1,0:T(8,128)}, u32[]{:S(2)}) copy-start(f32[256,1024]{1,0:T(8,128)} %param.26) | copy-start | bytes 3145732
  12.0 9.2 %copy-start.29 = (s32[1,512]{1,0:T(1,128)S(1)}, s32[1,512]{1,0:T(1,128)}, u32[]{:S(2)}) copy-start(s32[1,512]{1,0:T(1,128)} %param.21) | copy-start | bytes 6148
  12.0 51.8 %all-to-all-start = ((bf16[4,80,1792]{2,1,0:T(8,128)(2,1)}), bf16[4,80,1792]{2,1,0:T(8,128)(2,1)}, u32[]{:S(2)}, u32[]{:S(2)}) async-start(bf16[4,80,1792]{2,1,0:T(8,128)(2,1)} %pad_maximum_fusion), calls=%async_computation | async-start | bytes 2293760 | tf_op jit(solution)/shard_map/all_to_all | solution.py:354
  18.5 142.8 %reduce-scatter.5.cloned.1.call-start = ((), (), s32[]{:S(2)}) async-start(), calls=%async_computation.7 | async-start | bytes 1310720 | tf_op jit(solution)/shard_map/reduce_scatter | solution.py:403
  21.5 104.0 %copy-start.26 = (pred[512,512]{0,1:T(8,128)(4,1)}, pred[512,512]{0,1:T(8,128)(4,1)S(1)}, u32[]{:S(2)}) copy-start(pred[512,512]{0,1:T(8,128)(4,1)S(1)} %fusion.27) | copy-start | bytes 786436
  63.8 58.6 %copy-start.4 = (bf16[1,512,1024]{2,1,0:T(8,128)(2,1)S(1)}, bf16[1,512,1024]{2,1,0:T(8,128)(2,1)}, u32[]{:S(2)}) copy-start(bf16[1,512,1024]{2,1,0:T(8,128)(2,1)} %all-gather.11.cloned.1.call-done) | copy-start | bytes 3145732
  124.9 1.3 copy-start.22
  125.1 5.1 %copy-start.18 = (bf16[512,256]{0,1:T(8,128)(2,1)}, bf16[512,256]{0,1:T(8,128)(2,1)S(1)}, u32[]{:S(2)}) copy-start(bf16[512,256]{0,1:T(8,128)(2,1)S(1)} %copy.62) | copy-start | bytes 786436
  125.3 5.0 %copy-start.20 = (bf16[512,256]{0,1:T(8,128)(2,1)}, bf16[512,256]{0,1:T(8,128)(2,1)S(1)}, u32[]{:S(2)}) copy-start(bf16[512,256]{0,1:T(8,128)(2,1)S(1)} %copy.61) | copy-start | bytes 786436
  125.5 4.8 %copy-start.27 = (bf16[512,256]{0,1:T(8,128)(2,1)}, bf16[512,256]{0,1:T(8,128)(2,1)S(1)}, u32[]{:S(2)}) copy-start(bf16[512,256]{0,1:T(8,128)(2,1)S(1)} %copy.60) | copy-start | bytes 786436
  133.5 27.8 %copy-start = (bf16[1,128,1024]{2,1,0:T(8,128)(2,1)S(1)}, bf16[1,128,1024]{2,1,0:T(8,128)(2,1)}, u32[]{:S(2)}) copy-start(bf16[1,128,1024]{2,1,0:T(8,128)(2,1)} %param.19) | copy-start | bytes 786436
  136.1 56.1 %all-gather.7.cloned.1.call-start = ((), (), s32[]{:S(2)}) async-start(), calls=%async_computation.8 | async-start | bytes 1310720 | tf_op jit(solution)/shard_map/all_gather | solution.py:410
  165.4 55.7 %all-gather.13.cloned.1.call-start = ((), (), s32[]{:S(2)}) async-start(), calls=%async_computation.14 | async-start | bytes 1310720 | tf_op jit(solution)/shard_map/all_gather | solution.py:336
  166.0 90.7 %reduce-scatter.7.cloned.1.call-start = ((), (), s32[]{:S(2)}) async-start(), calls=%async_computation.9 | async-start | bytes 1310720 | tf_op jit(solution)/shard_map/reduce_scatter | solution.py:417
  221.1 6.5 %copy-start.32 = (bf16[4,4,64,1024]{3,2,1,0:T(8,128)(2,1)S(1)}, bf16[4,4,64,1024]{3,2,1,0:T(8,128)(2,1)}, u32[]{:S(2)}) copy-start(bf16[4,4,64,1024]{3,2,1,0:T(8,128)(2,1)} %get-tuple-element.32) | copy-start | bytes 6291460
  226.6 1.0 copy-start.36
  227.6 29.1 %copy-start.1 = (bf16[128,1024]{1,0:T(8,128)(2,1)S(1)}, bf16[128,1024]{1,0:T(8,128)(2,1)}, u32[]{:S(2)}) copy-start(bf16[128,1024]{1,0:T(8,128)(2,1)} %reduce-scatter.5.cloned.1.call-done) | copy-start | bytes 786436
  229.8 29.4 %copy-start.9 = (bf16[1,128,1024]{2,1,0:T(8,128)(2,1)S(1)}, bf16[1,128,1024]{2,1,0:T(8,128)(2,1)}, u32[]{:S(2)}) copy-start(bf16[1,128,1024]{2,1,0:T(8,128)(2,1)} %param.20) | copy-start | bytes 786436
  229.9 74.2 %all-gather.9.cloned.1.call-start = ((), (), s32[]{:S(2)}) async-start(), calls=%async_computation.10 | async-start | bytes 1310720 | tf_op jit(solution)/shard_map/all_gather | solution.py:425
  260.2 3.0 copy-start.34
  260.2 3.0 copy-start.35
  295.6 28.7 %all-to-all-start.2 = ((bf16[4,64,1024]{2,1,0:T(8,128)(2,1)}), bf16[4,64,1024]{2,1,0:T(8,128)(2,1)S(1)}, u32[]{:S(2)}, u32[]{:S(2)}) async-start(bf16[4,64,1024]{2,1,0:T(8,128)(2,1)} %get-tuple-element.39), calls=%async_computation.6 | async-start | bytes 1048576 | tf_op jit(solution)/shard_map/all_to_all | solution.py:509
  299.1 49.3 %reduce-scatter.11.cloned.1.call-start = ((), (), s32[]{:S(2)}) async-start(), calls=%async_computation.12 | async-start | bytes 1310720 | tf_op jit(solution)/shard_map/reduce_scatter | solution.py:468
  311.1 3.6 copy-start.2
  314.7 1.2 copy-start.21
  315.9 1.0 copy-start.19
  315.9 2.1 copy-start.24
  315.9 2.1 copy-start.33
  316.8 0.7 copy-start.14
  317.3 0.7 copy-start.16
  320.1 57.4 %reduce-scatter.9.cloned.1.call-start = ((), (), s32[]{:S(2)}) async-start(), calls=%async_computation.11 | async-start | bytes 1310720 | tf_op jit(solution)/shard_map/reduce_scatter | solution.py:429
  324.3 1.2 copy-start.12
  324.3 1.5 copy-start.13
  325.9 2.2 copy-start.8
  325.9 2.3 copy-start.15
  325.9 2.3 copy-start.17
  325.9 2.3 copy-start.25
  371.1 6.4 %copy-start.6 = (bf16[128,1024]{1,0:T(8,128)(2,1)S(1)}, bf16[128,1024]{1,0:T(8,128)(2,1)}, u32[]{:S(2)}) copy-start(bf16[128,1024]{1,0:T(8,128)(2,1)} %reduce-scatter.11.cloned.1.call-done) | copy-start | bytes 786436
  371.1 6.4 %copy-start.10 = (bf16[1,128,1024]{2,1,0:T(8,128)(2,1)S(1)}, bf16[1,128,1024]{2,1,0:T(8,128)(2,1)}, u32[]{:S(2)}) copy-start(bf16[1,128,1024]{2,1,0:T(8,128)(2,1)} %param.20) | copy-start | bytes 786436
  371.9 18.0 %all-to-all-start.1 = ((bf16[4,80,768]{2,1,0:T(8,128)(2,1)}), bf16[4,80,768]{2,1,0:T(8,128)(2,1)S(1)}, u32[]{:S(2)}, u32[]{:S(2)}) async-start(bf16[4,80,768]{2,1,0:T(8,128)(2,1)} %fusion.46), calls=%async_computation.5 | async-start | bytes 983040 | tf_op jit(solution)/shard_map/all_to_all | solution.py:513
  389.9 0.8 copy-start.11
  391.1 1.7 copy-start.28
  391.1 1.7 copy-start.30
  391.1 1.7 copy-start.31
  391.1 2.3 copy-start.7
Sparse Core Ops, SparseCore 0:
  9.6 51.0 all-gather.10
  136.2 25.0 reduce-scatter.4
  165.5 26.5 all-gather.6
  193.6 27.4 all-gather.12
  230.0 26.6 reduce-scatter.6
  260.2 26.5 all-gather.8
  320.2 28.1 reduce-scatter.10
  350.8 25.7 reduce-scatter.8

commit v3 on v2

--- a/solution.py
+++ b/solution.py
@@ -274,7 +274,11 @@
         compiler_params=pltpu.CompilerParams(
             collective_id=name, has_side_effects=True, vmem_limit_bytes=24 * 1024 * 1024
         ),
-        cost_estimate=pl.CostEstimate(flops=0, bytes_accessed=100_000_000, transcendentals=0),
+        cost_estimate=pl.CostEstimate(
+            flops=0,
+            bytes_accessed=20_000_000 + 20 * sum(item.size for item in arrays),
+            transcendentals=0,
+        ),
     )(*arrays)
 
 
@@ -332,9 +336,8 @@
     place_loc = own * length + jnp.arange(length, dtype=jnp.int32)
     live_loc = place_loc < row_fill[0]
 
-    rows_all = lax.all_gather(tokens_loc, "ctx", axis=0, tiled=True).astype(jnp.float32)
+    rows_all = lax.all_gather(tokens_loc, "ctx", axis=0, tiled=True)
     dy_all = lax.all_gather(grads_loc, "ctx", axis=0, tiled=True)
-    dy_all = jnp.where(live_all[:, None], dy_all, jnp.zeros_like(dy_all))
 
     vec_tile = jnp.pad(vectors.astype(jnp.bfloat16), (0, 2048 - vec_len)).reshape(16, 128)
     vec_tile = jnp.pad(vec_tile, ((0, 0), (0, wide_qkv + hid - 128)))
@@ -363,6 +366,11 @@
         (True, False, True, False, True),
         group,
     )
+    rows_all, dy_all, mat_qkv, vec_full = lax.optimization_barrier(
+        (rows_all, dy_all, mat_qkv, vec_full)
+    )
+    rows_all = rows_all.astype(jnp.float32)
+    dy_all = jnp.where(live_all[:, None], dy_all, jnp.zeros_like(dy_all))
     mat_qkv = mat_qkv.reshape(MODEL_WIDTH, wide_qkv)
     mat_up = mat_up.reshape(MODEL_WIDTH, hid)
     mat_down = mat_down.reshape(hid, MODEL_WIDTH)
@@ -491,7 +499,7 @@
     vec_pack = jnp.pad(
         grad_vec.reshape(parts, group, vec_len), ((0, 0), (0, 0), (0, 2048 - vec_len))
     ).reshape(parts, group, 16, 128)
-    sum_qkv, sum_out, sum_vec = reduce_all(
+    sum_qkv, sum_out = reduce_all(
         [
             outer_sum(hidden_one, grad_qkv_low)
             .astype(jnp.bfloat16)
@@ -499,35 +507,26 @@
             outer_sum(attn_mix, grad_attn)
             .astype(jnp.bfloat16)
             .reshape(group, 2, rows_out // 2, MODEL_WIDTH),
-            vec_pack.astype(jnp.bfloat16),
         ],
-        (True, False, True),
+        (True, False),
         group,
         2,
     )
+    (sum_vec,) = reduce_all([vec_pack.astype(jnp.bfloat16)], (True,), group, 3)
 
     ffn_cols = lax.all_to_all(sum_up, "ctx", 0, 0)
     total_up = ffn_cols.transpose(1, 0, 2).reshape(w_up.shape).astype(jnp.float32)
     total_down = sum_down.reshape(w_down.shape).astype(jnp.float32)
     total_out = sum_out.reshape(w_attn_out.shape).astype(jnp.float32)
-    qkv_cols = lax.all_to_all(
-        jnp.concatenate(
-            [sum_qkv, jnp.pad(sum_vec, ((0, 0), (0, 0), (0, wide_qkv - 128)))], axis=1
-        ),
-        "ctx",
-        0,
-        0,
-    )
+    qkv_cols = lax.all_to_all(sum_qkv, "ctx", 0, 0)
+    vec_cols = lax.all_to_all(sum_vec, "ctx", 0, 0)
     total_qkv = (
-        qkv_cols[:, :rows_in]
-        .reshape(parts, rows_in, 3, block)
+        qkv_cols.reshape(parts, rows_in, 3, block)
         .transpose(1, 2, 0, 3)
         .reshape(w_qkv.shape)
         .astype(jnp.float32)
     )
-    total_vec = jnp.sum(qkv_cols[:, rows_in:, :128].astype(jnp.float32), axis=0).reshape(-1)[
-        :vec_len
-    ]
+    total_vec = jnp.sum(vec_cols.astype(jnp.float32), axis=0).reshape(-1)[:vec_len]
     new_qkv, mom_qkv, sec_qkv = adamw_update(
         w_qkv, total_qkv, momentum_qkv_weight, second_qkv, 0.05, 0.1
     )

time: 405 us -> 372 us (0.919)
  waiting for transfers between devices: 168 us -> 128 us
  Pallas kernels: 102 us -> 109 us
  matrix products: 51.9 us -> 47.1 us
  starting transfers between devices: 14.1 us -> 18.5 us
    all_to_all x1, waiting for transfers between devices: 0.01 us -> 40.9 us  [shards(): cols = lax.all_to_all(send, 'ctx', 0, 0)]
    all_gather x1, waiting for transfers between devices: 39.3 us -> 0.02 us  [shards(): rows_all = lax.all_gather(tokens_loc, 'ctx', axis=0, tiled=True)]
    all_gather x1, waiting for transfers between devices: 24.3 us -> 0.02 us  [shards(): dy_all = lax.all_gather(grads_loc, 'ctx', axis=0, tiled=True)]
    reduce_scatter x1, waiting for transfers between devices: 15.3 us -> 0.01 us  [shards(): lax.psum_scatter(grad_first_part, 'ctx', scatter_dimension=0, tiled=True)]
    pallas_call x2 -> x3, Pallas kernels: 49.5 us -> 56.8 us  [reduce_over_group(): pl.pallas_call(functools.partial(reduce_kernel, group, kinds), out_shape=...]
    all_to_all x1 -> x2, starting transfers between devices: 3.47 us -> 8.04 us  [the longest x1 4.79 us: shards(): qkv_cols = lax.all_to_all(sum_qkv, 'ctx', 0, 0)]
    all_to_all x1 -> x2, waiting for transfers between devices: 10.3 us -> 7.12 us  [the longest x1 5.68 us: shards(): qkv_cols = lax.all_to_all(sum_qkv, 'ctx', 0, 0)]
  transfers between devices with their start and end apart: 11 -> 12, of which waited for: 7 -> 7; matrix products, arithmetic and copies ran while one was open for 15% -> 16% of each run, Pallas kernels for 12% -> 29%
where the time goes in v3:
time: 372 us; the launch traced here: 371 us
  waiting for transfers between devices  128 us (34%)
  Pallas kernels  109 us (29%)
  matrix products  47.1 us (13%)
  other arithmetic  39.8 us (11%)
  starting transfers between devices  18.5 us (5%)
  between operations  15.8 us (4%)
  local copies, waits for them, and re-layouts  12.1 us (3%)
    pallas_call x3, Pallas kernels, reduce_over_group(): pl.pallas_call(functools.partial(reduce_kernel, group, kinds), out_shape=...  56.8 us
    pallas_call x1, Pallas kernels, gather_over_group(): pl.pallas_call(functools.partial(gather_kernel, group, kinds), out_shape=...  52.3 us
    all_to_all x1, waiting for transfers between devices, shards(): cols = lax.all_to_all(send, 'ctx', 0, 0)  40.9 us
    reduce_scatter x1, waiting for transfers between devices, shards(): lax.psum_scatter(grad_normed_part, 'ctx', scatter_dimension=0, tiled=True)  26.7 us
    all_gather x1, waiting for transfers between devices, shards(): lax.all_gather(normed_two.astype(jnp.bfloat16), 'ctx', axis=0, tiled=True)  25.8 us
    reduce_scatter x1, waiting for transfers between devices, shards(): lax.psum_scatter(attn_part.astype(jnp.bfloat16), 'ctx', scatter_dimension...  24.5 us
    sub x5, other arithmetic, adamw_update(): weight - step_rate * (first_hat / (jnp.sqrt(second_hat) + adam_eps) + dec...  13 us
    dot_general x4, matrix products, times_trans(): lax.dot_general(left_mat, right_mat, (((1,), (1,)), ((), ())), preferred_...  11 us
  transfers between devices with their start and end apart: 12, of which 7 were waited for; matrix products, arithmetic and copies ran while one was open for 16% of the time, Pallas kernels for 29%

profile of v3, /device:TPU:0, one launch (start us, length us, event | category | flops | bytes accessed | tf_op | source)
XLA Modules:
  0.0 370.8 jit_solution(12109250143985674716)
XLA Ops:
  8.6 1.2 convert_element_type.174
  12.1 6.3 %all-to-all-start = ((bf16[4,80,1792]{2,1,0:T(8,128)(2,1)}), bf16[4,80,1792]{2,1,0:T(8,128)(2,1)S(1)}, u32[]{:S(2)}, u32[]{:S(2)}) async-start(bf16[4,80,1792]{2,1,0:T(8,128)(2,1)} %pad_maximum_fusion), calls=%async_computation | async-start | bytes 2293760 | tf_op jit(solution)/shard_map/all_to_all | solution.py:357
  22.2 40.9 %all-to-all-done = bf16[4,80,1792]{2,1,0:T(8,128)(2,1)S(1)} async-done(((bf16[4,80,1792]{2,1,0:T(8,128)(2,1)}), bf16[4,80,1792]{2,1,0:T(8,128)(2,1)S(1)}, u32[]{:S(2)}, u32[]{:S(2)}) %all-to-all-start) | async-done | bytes 1146912 | tf_op jit(solution)/shard_map/all_to_all | solution.py:357
  65.3 52.3 %shard_map.314 = (bf16[4,4,64,768]{3,2,1,0:T(8,128)(2,1)}, bf16[4,2,32,1024]{3,2,1,0:T(8,128)(2,1)}, bf16[4,4,64,1024]{3,2,1,0:T(8,128)(2,1)}, bf16[4,4,64,1024]{3,2,1,0:T(8,128)(2,1)}, bf16[4,4,16,128]{3,2,1,0:T(8,128)(2,1)}) custom-call(bf16[4,64,768]{2,1,0:T(8,128)(2,1)} %slice.69.refs_0_, bf16[2,32,1024]{2,1,0:T(8,128)(2,1)} %bitcast.197, ...), custom_call_target="tpu_custom_call" | custom-call | bytes 120000000 | tf_op jit(solution)/shard_map/pallas_call | solution.py:157
  118.7 1.4 convert_reduce_fusion
  120.1 1.6 fusion.4
  122.6 2.5 add_convert_fusion
  126.6 3.9 %fusion.75 = (f32[4,512]{1,0:T(4,128)S(1)}, f32[4,512,512]{1,2,0:T(8,128)}) fusion(f32[512,512]{0,1:T(8,128)S(1)} %copy-done.17, f32[4]{0:T(128)S(1)} %dynamic_slice.10, pred[512,512]{0,1:T(8,128)(4,1)S(1)} %fusion.26, bf16[512,4,64]{0,2,1:T(8,128)(2,1)S(1)} %bitcast.191, bf16[512,4,64]{0,2,1:T(8,128)(2,1)S(1)} %bitcast.187), kind=kOutput, calls=%fused_computation.159 | convolution fusion | flops 140509696 | bytes 6037520 | tf_op jit(solution)/shard_map/sub | solution.py:405
  130.5 3.4 convolution_convert_fusion.10
  133.9 1.4 convolution_convert_fusion.6
  135.4 24.5 %reduce-scatter.5.cloned.1.call-done = bf16[128,1024]{1,0:T(8,128)(2,1)} async-done(((bf16[512,1024]{1,0:T(8,128)(2,1)}), bf16[128,1024]{1,0:T(8,128)(2,1)}) %reduce-scatter.5.cloned.1.call-update) | async-done | bytes 262160 | tf_op jit(solution)/shard_map/reduce_scatter | solution.py:411
  162.2 1.8 add_convert_fusion.2
  164.9 25.8 %all-gather.7.cloned.1.call-done = bf16[512,1024]{1,0:T(8,128)(2,1)} async-done(((bf16[128,1024]{1,0:T(8,128)(2,1)}), bf16[512,1024]{1,0:T(8,128)(2,1)}) %all-gather.7.cloned.1.call-update) | async-done | bytes 1048592 | tf_op jit(solution)/shard_map/all_gather | solution.py:418
  190.7 3.3 fusion.76
  194.1 3.2 convert_reduce_fusion.1
  198.3 2.3 convolution_convert_fusion.5
  200.7 26.7 %reduce-scatter.7.cloned.1.call-done = bf16[128,1024]{1,0:T(8,128)(2,1)} async-done(((bf16[512,1024]{1,0:T(8,128)(2,1)}), bf16[128,1024]{1,0:T(8,128)(2,1)}) %reduce-scatter.7.cloned.1.call-update) | async-done | bytes 262160 | tf_op jit(solution)/shard_map/reduce_scatter | solution.py:425
  227.4 1.9 fusion.40
  229.3 1.3 fusion.71
  230.6 1.4 fusion.63
  232.7 3.0 convolution_convert_fusion.1
  235.7 1.7 convolution_convert_fusion
  237.4 30.6 %shard_map.316 = (bf16[4,64,1024]{2,1,0:T(8,128)(2,1)}, bf16[4,64,1024]{2,1,0:T(8,128)(2,1)S(1)}) custom-call(bf16[4,4,64,1024]{3,2,1,0:T(8,128)(2,1)S(1)} %bitcast.165, bf16[4,4,64,1024]{3,2,1,0:T(8,128)(2,1)S(1)} %bitcast.166), custom_call_target="tpu_custom_call" | custom-call | bytes 61943040 | tf_op jit(solution)/shard_map/pallas_call | solution.py:261
  268.0 3.5 all-to-all-start.2
  271.8 4.8 %convolution_convert_fusion.4 = bf16[512,1024]{1,0:T(8,128)(2,1)} fusion(bf16[1024,1024]{1,0:T(8,128)(2,1)} %bitcast.211, f32[512,1024]{1,0:T(8,128)} %copy-done.49, f32[1024]{0:T(1024)S(1)} %dynamic_slice.11), kind=kOutput, calls=%fused_computation.42 | convolution fusion | flops 1079508992 | bytes 5246976 | tf_op jit(solution)/shard_map/dot_general | solution.py:435
  276.6 1.8 convolution_convert_fusion.9
  278.5 3.2 multiply_reduce_fusion
  282.1 1.2 multiply_convert_fusion
  283.3 1.5 fusion.20
  284.7 1.2 fusion.19
  285.9 4.5 %convolution_convert_fusion.8 = bf16[4,64,512]{2,1,0:T(8,128)(2,1)} fusion(bf16[512,4,64]{0,2,1:T(8,128)(2,1)} %bitcast.220, f32[4,512]{1,0:T(4,128)S(1)} %get-tuple-element.88, f32[512,512]{0,1:T(8,128)} %subtract_convert_fusion, f32[4]{0:T(128)S(1)} %dynamic_slice.10, pred[512,512]{0,1:T(8,128)(4,1)} %copy-done.22, bf16[512,4,64]{0,2,1:T(8,128)(2,1)} %bitcast.193, ...), kind=kOutput, calls=%fused_computation.48 | convolution fusion | flops 275909120 | bytes 2367504 | tf_op jit(solution)/shard_map/hqk,qhd->khd/dot_general | solution.py:455
  290.4 3.7 convolution_convert_fusion.3
  294.1 4.2 %multiply_subtract_fusion = (f32[256,1024]{1,0:T(8,128)}, f32[256,1024]{1,0:T(8,128)}, f32[256,1024]{1,0:T(8,128)}) fusion(f32[256,1024]{1,0:T(8,128)} %param.26, bf16[4,64,1024]{2,1,0:T(8,128)(2,1)S(1)} %get-tuple-element.46, f32[256,1024]{1,0:T(8,128)} %param.31, f32[256,1024]{1,0:T(8,128)} %param.36), kind=kLoop, calls=%fused_computation.59 | loop fusion | flops 4194304 | bytes 6815744 | tf_op jit(solution)/shard_map/sub | solution.py:78
  300.1 1.3 convolution_convert_fusion.2
  301.4 19.5 %shard_map.315 = (bf16[4,64,768]{2,1,0:T(8,128)(2,1)}, bf16[2,32,1024]{2,1,0:T(8,128)(2,1)S(1)}) custom-call(bf16[4,4,64,768]{3,2,1,0:T(8,128)(2,1)S(1)} %bitcast.168, bf16[4,2,32,1024]{3,2,1,0:T(8,128)(2,1)S(1)} %bitcast.167), custom_call_target="tpu_custom_call" | custom-call | bytes 40971520 | tf_op jit(solution)/shard_map/pallas_call | solution.py:261
  320.9 4.8 %all-to-all-start.1 = ((bf16[4,64,768]{2,1,0:T(8,128)(2,1)}), bf16[4,64,768]{2,1,0:T(8,128)(2,1)}, u32[]{:S(2)}, u32[]{:S(2)}) async-start(bf16[4,64,768]{2,1,0:T(8,128)(2,1)} %get-tuple-element.43), calls=%async_computation.5 | async-start | bytes 786432 | tf_op jit(solution)/shard_map/all_to_all | solution.py:521
  325.7 3.8 %multiply_subtract_fusion.1 = (f32[64,4096]{1,0:T(8,128)}, f32[64,4096]{1,0:T(8,128)}, f32[64,4096]{1,0:T(8,128)}) fusion(f32[64,4096]{1,0:T(8,128)S(1)} %copy-done.3, f32[64,4096]{1,0:T(8,128)S(1)} %bitcast.169, f32[64,4096]{1,0:T(8,128)} %param.30, f32[64,4096]{1,0:T(8,128)} %param.35), kind=kLoop, calls=%fused_computation.60 | loop fusion | flops 3932160 | bytes 7340032 | tf_op jit(solution)/shard_map/sub | solution.py:78
  329.5 1.4 convert_reduce_fusion.2
  332.3 5.7 %all-to-all-done.1 = bf16[4,64,768]{2,1,0:T(8,128)(2,1)} async-done(((bf16[4,64,768]{2,1,0:T(8,128)(2,1)}), bf16[4,64,768]{2,1,0:T(8,128)(2,1)}, u32[]{:S(2)}, u32[]{:S(2)}) %all-to-all-start.1) | async-done | bytes 393248 | tf_op jit(solution)/shard_map/all_to_all | solution.py:521
  338.0 1.5 reshape.335
  340.5 3.4 multiply_subtract_fusion.2
  345.0 1.2 fusion.42
  346.2 1.3 fusion.41
  347.8 6.7 %shard_map.317 = bf16[4,16,128]{2,1,0:T(8,128)(2,1)} custom-call(bf16[4,4,16,128]{3,2,1,0:T(8,128)(2,1)S(1)} %convert_element_type.224.refs_0_), custom_call_target="tpu_custom_call" | custom-call | bytes 20655360 | tf_op jit(solution)/shard_map/pallas_call | solution.py:261
  354.5 3.3 all-to-all-start.3
  357.8 1.9 reduce-scatter.9.cloned.1.call-done
  359.7 2.2 add_bitcast_fusion
  361.9 1.4 all-to-all-done.3
  (199 shorter events, 23.8 us)
Async XLA Ops:
  7.2 3.6 copy-start.3
  7.2 110.5 %all-gather.13.cloned.1.call-start = ((), (), s32[]{:S(2)}) async-start(), calls=%async_computation.15 | async-start | bytes 1310720 | tf_op jit(solution)/shard_map/all_gather | solution.py:340
  10.9 8.3 %copy-start.18 = (f32[64,1024]{1,0:T(8,128)S(1)}, f32[64,1024]{1,0:T(8,128)}, u32[]{:S(2)}) copy-start(f32[64,1024]{1,0:T(8,128)} %param.24) | copy-start | bytes 786436
  10.9 8.9 %copy-start.6 = (f32[256,1024]{1,0:T(8,128)S(1)}, f32[256,1024]{1,0:T(8,128)}, u32[]{:S(2)}) copy-start(f32[256,1024]{1,0:T(8,128)} %param.26) | copy-start | bytes 3145732
  12.1 51.0 %all-to-all-start = ((bf16[4,80,1792]{2,1,0:T(8,128)(2,1)}), bf16[4,80,1792]{2,1,0:T(8,128)(2,1)S(1)}, u32[]{:S(2)}, u32[]{:S(2)}) async-start(bf16[4,80,1792]{2,1,0:T(8,128)(2,1)} %pad_maximum_fusion), calls=%async_computation | async-start | bytes 2293760 | tf_op jit(solution)/shard_map/all_to_all | solution.py:357
  18.4 3.5 copy-start.27
  18.4 99.3 %all-gather.11.cloned.1.call-start = ((), (), s32[]{:S(2)}) async-start(), calls=%async_computation.14 | async-start | bytes 1310720 | tf_op jit(solution)/shard_map/all_gather | solution.py:339
  19.1 140.7 %reduce-scatter.5.cloned.1.call-start = ((), (), s32[]{:S(2)}) async-start(), calls=%async_computation.8 | async-start | bytes 1310720 | tf_op jit(solution)/shard_map/reduce_scatter | solution.py:411
  22.2 104.3 %copy-start.22 = (pred[512,512]{0,1:T(8,128)(4,1)}, pred[512,512]{0,1:T(8,128)(4,1)S(1)}, u32[]{:S(2)}) copy-start(pred[512,512]{0,1:T(8,128)(4,1)S(1)} %fusion.26) | copy-start | bytes 786436
  117.7 4.9 %copy-start.4 = (bf16[1,512,1024]{2,1,0:T(8,128)(2,1)S(1)}, bf16[1,512,1024]{2,1,0:T(8,128)(2,1)}, u32[]{:S(2)}) copy-start(bf16[1,512,1024]{2,1,0:T(8,128)(2,1)} %all-gather.11.cloned.1.call-done) | copy-start | bytes 3145732
  120.1 5.1 %copy-start.28 = (f32[512]{0:T(512)}, f32[512]{0:T(512)S(1)}, u32[]{:S(2)}) copy-start(f32[512]{0:T(512)S(1)} %broadcast_multiply_fusion) | copy-start | bytes 6148
  121.8 3.4 copy-start.38
  125.4 5.1 %copy-start.13 = (bf16[512,256]{0,1:T(8,128)(2,1)}, bf16[512,256]{0,1:T(8,128)(2,1)S(1)}, u32[]{:S(2)}) copy-start(bf16[512,256]{0,1:T(8,128)(2,1)S(1)} %copy.62) | copy-start | bytes 786436
  125.6 4.9 %copy-start.15 = (bf16[512,256]{0,1:T(8,128)(2,1)}, bf16[512,256]{0,1:T(8,128)(2,1)S(1)}, u32[]{:S(2)}) copy-start(bf16[512,256]{0,1:T(8,128)(2,1)S(1)} %copy.61) | copy-start | bytes 786436
  130.5 3.4 copy-start.20
  133.9 26.0 %copy-start = (bf16[1,128,1024]{2,1,0:T(8,128)(2,1)S(1)}, bf16[1,128,1024]{2,1,0:T(8,128)(2,1)}, u32[]{:S(2)}) copy-start(bf16[1,128,1024]{2,1,0:T(8,128)(2,1)} %param.19) | copy-start | bytes 786436
  135.3 55.4 %all-gather.7.cloned.1.call-start = ((), (), s32[]{:S(2)}) async-start(), calls=%async_computation.9 | async-start | bytes 1310720 | tf_op jit(solution)/shard_map/all_gather | solution.py:418
  164.0 63.4 %reduce-scatter.7.cloned.1.call-start = ((), (), s32[]{:S(2)}) async-start(), calls=%async_computation.10 | async-start | bytes 1310720 | tf_op jit(solution)/shard_map/reduce_scatter | solution.py:425
  190.7 3.3 copy-start.44
  190.7 3.3 copy-start.46
  194.1 3.3 copy-start.49
  194.1 4.2 %copy-start.45 = (bf16[4,4,64,1024]{3,2,1,0:T(8,128)(2,1)S(1)}, bf16[4,4,64,1024]{3,2,1,0:T(8,128)(2,1)}, u32[]{:S(2)}) copy-start(bf16[4,4,64,1024]{3,2,1,0:T(8,128)(2,1)} %get-tuple-element.38) | copy-start | bytes 6291460
  198.3 29.1 %copy-start.1 = (bf16[128,1024]{1,0:T(8,128)(2,1)S(1)}, bf16[128,1024]{1,0:T(8,128)(2,1)}, u32[]{:S(2)}) copy-start(bf16[128,1024]{1,0:T(8,128)(2,1)} %reduce-scatter.5.cloned.1.call-done) | copy-start | bytes 786436
  200.6 30.0 %copy-start.8 = (bf16[1,128,1024]{2,1,0:T(8,128)(2,1)S(1)}, bf16[1,128,1024]{2,1,0:T(8,128)(2,1)}, u32[]{:S(2)}) copy-start(bf16[1,128,1024]{2,1,0:T(8,128)(2,1)} %param.20) | copy-start | bytes 786436
  200.6 76.0 %all-gather.9.cloned.1.call-start = ((), (), s32[]{:S(2)}) async-start(), calls=%async_computation.11 | async-start | bytes 1310720 | tf_op jit(solution)/shard_map/all_gather | solution.py:433
  200.7 35.0 %copy-start.40 = (pred[128]{0:T(512)(128)(4,1)}, pred[128]{0:T(512)(128)(4,1)S(1)}, u32[]{:S(2)}) copy-start(pred[128]{0:T(512)(128)(4,1)S(1)} %add_compare_fusion) | copy-start | bytes 388
  230.5 5.1 %copy-start.42 = (f32[128]{0:T(128)}, f32[128]{0:T(128)S(1)}, u32[]{:S(2)}) copy-start(f32[128]{0:T(128)S(1)} %negate_multiply_fusion.1) | copy-start | bytes 1540
  232.7 3.0 copy-start.47
  232.7 3.0 copy-start.50
  268.0 30.2 %all-to-all-start.2 = ((bf16[4,64,1024]{2,1,0:T(8,128)(2,1)}), bf16[4,64,1024]{2,1,0:T(8,128)(2,1)S(1)}, u32[]{:S(2)}, u32[]{:S(2)}) async-start(bf16[4,64,1024]{2,1,0:T(8,128)(2,1)} %get-tuple-element.45), calls=%async_computation.6 | async-start | bytes 1048576 | tf_op jit(solution)/shard_map/all_to_all | solution.py:517
  271.5 72.4 %reduce-scatter.11.cloned.1.call-start = ((), (), s32[]{:S(2)}) async-start(), calls=%async_computation.13 | async-start | bytes 1310720 | tf_op jit(solution)/shard_map/reduce_scatter | solution.py:476
  278.4 3.2 copy-start.48
  278.5 3.6 copy-start.2
  320.9 17.1 %all-to-all-start.1 = ((bf16[4,64,768]{2,1,0:T(8,128)(2,1)}), bf16[4,64,768]{2,1,0:T(8,128)(2,1)}, u32[]{:S(2)}, u32[]{:S(2)}) async-start(bf16[4,64,768]{2,1,0:T(8,128)(2,1)} %get-tuple-element.43), calls=%async_computation.5 | async-start | bytes 786432 | tf_op jit(solution)/shard_map/all_to_all | solution.py:521
  325.7 34.0 %reduce-scatter.9.cloned.1.call-start = ((), (), s32[]{:S(2)}) async-start(), calls=%async_computation.12 | async-start | bytes 1310720 | tf_op jit(solution)/shard_map/reduce_scatter | solution.py:437
  325.7 3.8 %copy-start.7 = (bf16[128,1024]{1,0:T(8,128)(2,1)S(1)}, bf16[128,1024]{1,0:T(8,128)(2,1)}, u32[]{:S(2)}) copy-start(bf16[128,1024]{1,0:T(8,128)(2,1)} %reduce-scatter.7.cloned.1.call-done) | copy-start | bytes 786436
  340.4 4.5 %copy-start.33 = (f32[128]{0:T(128)S(1)}, f32[128]{0:T(128)}, u32[]{:S(2)}) copy-start(f32[128]{0:T(128)} %broadcast_multiply_fusion.1) | copy-start | bytes 1540
  340.4 7.1 %copy-start.32 = (bf16[1024]{0:T(1024)(128)(2,1)S(1)}, bf16[1024]{0:T(1024)(128)(2,1)}, u32[]{:S(2)}) copy-start(bf16[1024]{0:T(1024)(128)(2,1)} %get-tuple-element.56) | copy-start | bytes 6148
  340.4 7.1 %copy-start.30 = (bf16[1024]{0:T(1024)(128)(2,1)S(1)}, bf16[1024]{0:T(1024)(128)(2,1)}, u32[]{:S(2)}) copy-start(bf16[1024]{0:T(1024)(128)(2,1)} %get-tuple-element.47) | copy-start | bytes 6148
  340.4 7.2 %copy-start.31 = (bf16[1024]{0:T(1024)(128)(2,1)S(1)}, bf16[1024]{0:T(1024)(128)(2,1)}, u32[]{:S(2)}) copy-start(bf16[1024]{0:T(1024)(128)(2,1)} %get-tuple-element.75) | copy-start | bytes 6148
  340.4 19.2 %copy-start.9 = (bf16[1,128,1024]{2,1,0:T(8,128)(2,1)S(1)}, bf16[1,128,1024]{2,1,0:T(8,128)(2,1)}, u32[]{:S(2)}) copy-start(bf16[1,128,1024]{2,1,0:T(8,128)(2,1)} %param.20) | copy-start | bytes 786436
  340.5 19.2 %copy-start.25 = (f32[1024]{0:T(1024)S(1)}, f32[1024]{0:T(1024)}, u32[]{:S(2)}) copy-start(f32[1024]{0:T(1024)} %get-tuple-element.80) | copy-start | bytes 12292
  340.5 19.2 %copy-start.41 = (pred[128]{0:T(512)(128)(4,1)S(1)}, pred[128]{0:T(512)(128)(4,1)}, u32[]{:S(2)}) copy-start(pred[128]{0:T(512)(128)(4,1)} %copy-done.40) | copy-start | bytes 388
  340.5 19.2 %copy-start.43 = (f32[128]{0:T(128)S(1)}, f32[128]{0:T(128)}, u32[]{:S(2)}) copy-start(f32[128]{0:T(128)} %copy-done.42) | copy-start | bytes 1540
  344.9 18.4 %copy-start.26 = (f32[832]{0:T(1024)S(1)}, f32[832]{0:T(1024)}, u32[]{:S(2)}) copy-start(f32[832]{0:T(1024)} %param.27) | copy-start | bytes 9988
  344.9 18.4 %copy-start.34 = (f32[832]{0:T(1024)S(1)}, f32[832]{0:T(1024)}, u32[]{:S(2)}) copy-start(f32[832]{0:T(1024)} %param.32) | copy-start | bytes 9988
  344.9 18.4 %copy-start.35 = (f32[832]{0:T(1024)S(1)}, f32[832]{0:T(1024)}, u32[]{:S(2)}) copy-start(f32[832]{0:T(1024)} %param.37) | copy-start | bytes 9988
  354.5 8.8 %all-to-all-start.3 = ((bf16[4,16,128]{2,1,0:T(8,128)(2,1)}), bf16[4,16,128]{2,1,0:T(8,128)(2,1)S(1)}, u32[]{:S(2)}, u32[]{:S(2)}) async-start(bf16[4,16,128]{2,1,0:T(8,128)(2,1)} %shard_map.317), calls=%async_computation.7 | async-start | bytes 32768 | tf_op jit(solution)/shard_map/all_to_all | solution.py:522
  (16 other events, 25.2 us)
Sparse Core Ops, SparseCore 0:
  9.6 50.9 all-gather.12
  62.2 27.8 all-gather.10
  135.5 24.3 reduce-scatter.4
  164.1 26.5 all-gather.6
  200.7 26.6 reduce-scatter.6
  232.1 26.5 all-gather.8
  294.2 28.1 reduce-scatter.10
  331.4 28.2 reduce-scatter.8

commit v4 on v3

--- a/solution.py
+++ b/solution.py
@@ -336,8 +336,6 @@
     place_loc = own * length + jnp.arange(length, dtype=jnp.int32)
     live_loc = place_loc < row_fill[0]
 
-    rows_all = lax.all_gather(tokens_loc, "ctx", axis=0, tiled=True)
-    dy_all = lax.all_gather(grads_loc, "ctx", axis=0, tiled=True)
 
     vec_tile = jnp.pad(vectors.astype(jnp.bfloat16), (0, 2048 - vec_len)).reshape(16, 128)
     vec_tile = jnp.pad(vec_tile, ((0, 0), (0, wide_qkv + hid - 128)))
@@ -355,6 +353,9 @@
         [send, jnp.broadcast_to(vec_tile[None], (parts,) + vec_tile.shape)], axis=1
     )
     cols = lax.all_to_all(send, "ctx", 0, 0)
+    cols, tokens_next, grads_next = lax.optimization_barrier((cols, tokens_loc, grads_loc))
+    rows_all = lax.all_gather(tokens_next, "ctx", axis=0, tiled=True)
+    dy_all = lax.all_gather(grads_next, "ctx", axis=0, tiled=True)
     mat_qkv, mat_out, mat_up, mat_down, vec_full = gather_all(
         [
             cols[:, :rows_in, :wide_qkv],

time: 372 us -> 352 us (0.946)
  waiting for transfers between devices: 128 us -> 86.8 us
  blocking collectives: 0 us -> 34.1 us
  starting transfers between devices: 18.5 us -> 12.3 us
  matrix products: 47.1 us -> 43.3 us
    all_to_all x1 -> x0, waiting for transfers between devices: 40.9 us -> none  [shards(): cols = lax.all_to_all(send, 'ctx', 0, 0)]
    all_to_all x0 -> x1, blocking collectives: none -> 34.1 us  [shards(): cols = lax.all_to_all(send, 'ctx', 0, 0)]
    all_to_all x1 -> x0, starting transfers between devices: 6.32 us -> none  [shards(): cols = lax.all_to_all(send, 'ctx', 0, 0)]
  transfers between devices with their start and end apart: 12 -> 11, of which waited for: 7 -> 6; matrix products, arithmetic and copies ran while one was open for 16% -> 15% of each run, Pallas kernels for 29% -> 31%
where the time goes in v4:
time: 352 us; the launch traced here: 351 us
  Pallas kernels  109 us (31%)
  waiting for transfers between devices  86.8 us (25%)
  matrix products  43.3 us (12%)
  other arithmetic  37.4 us (11%)
  blocking collectives  34.1 us (10%)
  between operations  15.7 us (4%)
  local copies, waits for them, and re-layouts  12.6 us (4%)
  starting transfers between devices  12.3 us (3%)
    pallas_call x3, Pallas kernels, reduce_over_group(): pl.pallas_call(functools.partial(reduce_kernel, group, kinds), out_shape=...  56.8 us
    pallas_call x1, Pallas kernels, gather_over_group(): pl.pallas_call(functools.partial(gather_kernel, group, kinds), out_shape=...  52.3 us
    all_to_all x1, blocking collectives, shards(): cols = lax.all_to_all(send, 'ctx', 0, 0)  34.1 us
    reduce_scatter x1, waiting for transfers between devices, shards(): lax.psum_scatter(grad_normed_part, 'ctx', scatter_dimension=0, tiled=True)  26.7 us
    all_gather x1, waiting for transfers between devices, shards(): lax.all_gather(normed_two.astype(jnp.bfloat16), 'ctx', axis=0, tiled=True)  25.8 us
    reduce_scatter x1, waiting for transfers between devices, shards(): lax.psum_scatter(attn_part.astype(jnp.bfloat16), 'ctx', scatter_dimension...  24.5 us
    sub x5, other arithmetic, adamw_update(): weight - step_rate * (first_hat / (jnp.sqrt(second_hat) + adam_eps) + dec...  12.5 us
    dot_general x4, matrix products, times_trans(): lax.dot_general(left_mat, right_mat, (((1,), (1,)), ((), ())), preferred_...  9.27 us
  transfers between devices with their start and end apart: 11, of which 6 were waited for; matrix products, arithmetic and copies ran while one was open for 15% of the time, Pallas kernels for 31%

profile of v4, /device:TPU:0, one launch (start us, length us, event | category | flops | bytes accessed | tf_op | source)
XLA Modules:
  0.0 351.4 jit_solution(5395641830624565691)
XLA Ops:
  8.0 1.2 convert_element_type.174
  10.4 34.1 %all_to_all.20 = bf16[4,80,1792]{2,1,0:T(8,128)(2,1)S(1)} all-to-all(bf16[4,80,1792]{2,1,0:T(8,128)(2,1)S(1)} %pad_maximum_fusion), channel_id=1, replica_groups=mesh['ctx'=4,'fsdp'=4,'replica'=2] {'ctx'}, dimensions={0} | all-to-all | bytes 2293760 | tf_op jit(solution)/shard_map/all_to_all | solution.py:355
  51.2 52.3 %shard_map.314 = (bf16[4,4,64,768]{3,2,1,0:T(8,128)(2,1)}, bf16[4,2,32,1024]{3,2,1,0:T(8,128)(2,1)}, bf16[4,4,64,1024]{3,2,1,0:T(8,128)(2,1)}, bf16[4,4,64,1024]{3,2,1,0:T(8,128)(2,1)}, bf16[4,4,16,128]{3,2,1,0:T(8,128)(2,1)}) custom-call(bf16[4,64,768]{2,1,0:T(8,128)(2,1)} %slice.52.refs_0_, bf16[2,32,1024]{2,1,0:T(8,128)(2,1)} %bitcast.169, ...), custom_call_target="tpu_custom_call" | custom-call | bytes 120000000 | tf_op jit(solution)/shard_map/pallas_call | solution.py:157
  104.6 1.4 convert_reduce_fusion
  106.0 1.6 fusion.4
  108.0 2.5 add_convert_fusion
  112.0 4.0 %fusion.73 = (f32[4,512]{1,0:T(4,128)S(1)}, f32[4,512,512]{1,2,0:T(8,128)}) fusion(f32[512,512]{0,1:T(8,128)S(1)} %copy-done.23, f32[4]{0:T(128)S(1)} %dynamic_slice.10, pred[512,512]{0,1:T(8,128)(4,1)S(1)} %copy-done.30, bf16[512,4,64]{0,2,1:T(8,128)(2,1)S(1)} %bitcast.163, bf16[512,4,64]{0,2,1:T(8,128)(2,1)S(1)} %bitcast.159), kind=kOutput, calls=%fused_computation.158 | convolution fusion | flops 140509696 | bytes 6037520 | tf_op jit(solution)/shard_map/sub | solution.py:406
  116.0 3.4 convolution_convert_fusion.10
  119.4 1.4 convolution_convert_fusion.6
  120.9 24.5 %reduce-scatter.5.cloned.1.call-done = bf16[128,1024]{1,0:T(8,128)(2,1)} async-done(((bf16[512,1024]{1,0:T(8,128)(2,1)}), bf16[128,1024]{1,0:T(8,128)(2,1)}) %reduce-scatter.5.cloned.1.call-update) | async-done | bytes 262160 | tf_op jit(solution)/shard_map/reduce_scatter | solution.py:412
  145.4 1.1 fusion.44
  146.5 1.2 multiply_reduce_fusion.1
  147.7 1.8 add_convert_fusion.2
  150.4 25.8 %all-gather.9.cloned.1.call-done = bf16[512,1024]{1,0:T(8,128)(2,1)} async-done(((bf16[128,1024]{1,0:T(8,128)(2,1)}), bf16[512,1024]{1,0:T(8,128)(2,1)}) %all-gather.9.cloned.1.call-update) | async-done | bytes 1048592 | tf_op jit(solution)/shard_map/all_gather | solution.py:419
  176.2 3.3 fusion.74
  179.6 3.3 convert_reduce_fusion.1
  183.8 2.3 convolution_convert_fusion.5
  186.2 26.7 %reduce-scatter.7.cloned.1.call-done = bf16[128,1024]{1,0:T(8,128)(2,1)} async-done(((bf16[512,1024]{1,0:T(8,128)(2,1)}), bf16[128,1024]{1,0:T(8,128)(2,1)}) %reduce-scatter.7.cloned.1.call-update) | async-done | bytes 262160 | tf_op jit(solution)/shard_map/reduce_scatter | solution.py:426
  212.9 1.3 fusion.38
  214.2 1.3 fusion.69
  216.4 3.0 convolution_convert_fusion.1
  219.5 1.7 convolution_convert_fusion
  221.2 30.6 %shard_map.316 = (bf16[4,64,1024]{2,1,0:T(8,128)(2,1)}, bf16[4,64,1024]{2,1,0:T(8,128)(2,1)S(1)}) custom-call(bf16[4,4,64,1024]{3,2,1,0:T(8,128)(2,1)S(1)} %bitcast.139, bf16[4,4,64,1024]{3,2,1,0:T(8,128)(2,1)S(1)} %bitcast.140), custom_call_target="tpu_custom_call" | custom-call | bytes 61943040 | tf_op jit(solution)/shard_map/pallas_call | solution.py:261
  251.8 3.5 all-to-all-start.2
  255.6 4.0 %multiply_subtract_fusion = (f32[256,1024]{1,0:T(8,128)}, f32[256,1024]{1,0:T(8,128)}, f32[256,1024]{1,0:T(8,128)}) fusion(f32[256,1024]{1,0:T(8,128)S(1)} %copy-done.9, bf16[4,64,1024]{2,1,0:T(8,128)(2,1)S(1)} %get-tuple-element.52, f32[256,1024]{1,0:T(8,128)} %param.31, f32[256,1024]{1,0:T(8,128)} %param.36), kind=kLoop, calls=%fused_computation.59 | loop fusion | flops 4194304 | bytes 6815744 | tf_op jit(solution)/shard_map/sub | solution.py:78
  259.6 2.5 convolution_convert_fusion.4
  262.1 1.7 convolution_convert_fusion.9
  263.9 3.1 multiply_reduce_fusion
  267.4 1.2 multiply_convert_fusion
  268.6 1.5 fusion.20
  270.1 4.5 %convolution_convert_fusion.8 = bf16[4,64,512]{2,1,0:T(8,128)(2,1)} fusion(bf16[512,4,64]{0,2,1:T(8,128)(2,1)} %bitcast.190, f32[4,512]{1,0:T(4,128)S(1)} %get-tuple-element.95, f32[512,512]{0,1:T(8,128)} %subtract_convert_fusion, f32[4]{0:T(128)S(1)} %dynamic_slice.10, pred[512,512]{0,1:T(8,128)(4,1)} %fusion.26, bf16[512,4,64]{0,2,1:T(8,128)(2,1)} %bitcast.165, ...), kind=kOutput, calls=%fused_computation.48 | convolution fusion | flops 275909120 | bytes 2367504 | tf_op jit(solution)/shard_map/hqk,qhd->khd/dot_general | solution.py:456
  274.5 1.6 fusion.19
  276.8 2.0 convolution_convert_fusion.3
  280.8 1.3 convolution_convert_fusion.2
  282.0 19.5 %shard_map.315 = (bf16[4,64,768]{2,1,0:T(8,128)(2,1)}, bf16[2,32,1024]{2,1,0:T(8,128)(2,1)S(1)}) custom-call(bf16[4,4,64,768]{3,2,1,0:T(8,128)(2,1)S(1)} %bitcast.142, bf16[4,2,32,1024]{3,2,1,0:T(8,128)(2,1)S(1)} %bitcast.141), custom_call_target="tpu_custom_call" | custom-call | bytes 40971520 | tf_op jit(solution)/shard_map/pallas_call | solution.py:261
  301.6 5.1 %all-to-all-start.1 = ((bf16[4,64,768]{2,1,0:T(8,128)(2,1)}), bf16[4,64,768]{2,1,0:T(8,128)(2,1)}, u32[]{:S(2)}, u32[]{:S(2)}) async-start(bf16[4,64,768]{2,1,0:T(8,128)(2,1)} %get-tuple-element.49), calls=%async_computation.5 | async-start | bytes 786432 | tf_op jit(solution)/shard_map/all_to_all | solution.py:522
  306.7 3.8 %multiply_subtract_fusion.1 = (f32[64,4096]{1,0:T(8,128)}, f32[64,4096]{1,0:T(8,128)}, f32[64,4096]{1,0:T(8,128)}) fusion(f32[64,4096]{1,0:T(8,128)S(1)} %copy-done.6, f32[64,4096]{1,0:T(8,128)S(1)} %bitcast.144, f32[64,4096]{1,0:T(8,128)} %param.30, f32[64,4096]{1,0:T(8,128)} %param.35), kind=kLoop, calls=%fused_computation.60 | loop fusion | flops 3932160 | bytes 7340032 | tf_op jit(solution)/shard_map/sub | solution.py:78
  310.5 1.4 convert_reduce_fusion.2
  313.3 5.6 %all-to-all-done.1 = bf16[4,64,768]{2,1,0:T(8,128)(2,1)} async-done(((bf16[4,64,768]{2,1,0:T(8,128)(2,1)}), bf16[4,64,768]{2,1,0:T(8,128)(2,1)}, u32[]{:S(2)}, u32[]{:S(2)}) %all-to-all-start.1) | async-done | bytes 393248 | tf_op jit(solution)/shard_map/all_to_all | solution.py:522
  318.9 1.5 reshape.335
  321.3 3.1 multiply_subtract_fusion.2
  325.6 1.2 fusion.40
  326.8 1.3 fusion.39
  328.4 6.7 %shard_map.317 = bf16[4,16,128]{2,1,0:T(8,128)(2,1)} custom-call(bf16[4,4,16,128]{3,2,1,0:T(8,128)(2,1)S(1)} %convert_element_type.224.refs_0_), custom_call_target="tpu_custom_call" | custom-call | bytes 20655360 | tf_op jit(solution)/shard_map/pallas_call | solution.py:261
  335.1 3.3 all-to-all-start.3
  338.4 2.2 reduce-scatter.9.cloned.1.call-done
  340.6 2.2 add_bitcast_fusion
  342.8 1.2 all-to-all-done.3
  (191 shorter events, 21.2 us)
Async XLA Ops:
  7.2 3.0 copy-start.5
  7.2 96.4 %all-gather.5.cloned.1.call-start = ((), (), s32[]{:S(2)}) async-start(), calls=%async_computation.8 | async-start | bytes 1310720 | tf_op jit(solution)/shard_map/all_gather | solution.py:357
  10.3 35.0 %copy-start.24 = (f32[64,1024]{1,0:T(8,128)S(1)}, f32[64,1024]{1,0:T(8,128)}, u32[]{:S(2)}) copy-start(f32[64,1024]{1,0:T(8,128)} %param.24) | copy-start | bytes 786436
  10.4 35.6 %copy-start.9 = (f32[256,1024]{1,0:T(8,128)S(1)}, f32[256,1024]{1,0:T(8,128)}, u32[]{:S(2)}) copy-start(f32[256,1024]{1,0:T(8,128)} %param.26) | copy-start | bytes 3145732
  44.5 3.6 %copy-start.35 = (s32[1,512]{1,0:T(1,128)S(1)}, s32[1,512]{1,0:T(1,128)}, u32[]{:S(2)}) copy-start(s32[1,512]{1,0:T(1,128)} %param.21) | copy-start | bytes 6148
  44.5 59.1 %all-gather.7.cloned.1.call-start = ((), (), s32[]{:S(2)}) async-start(), calls=%async_computation.9 | async-start | bytes 1310720 | tf_op jit(solution)/shard_map/all_gather | solution.py:358
  45.3 100.1 %reduce-scatter.5.cloned.1.call-start = ((), (), s32[]{:S(2)}) async-start(), calls=%async_computation.10 | async-start | bytes 1310720 | tf_op jit(solution)/shard_map/reduce_scatter | solution.py:412
  103.6 4.4 %copy-start.7 = (bf16[512,1024]{1,0:T(8,128)(2,1)S(1)}, bf16[512,1024]{1,0:T(8,128)(2,1)}, u32[]{:S(2)}) copy-start(bf16[512,1024]{1,0:T(8,128)(2,1)} %all-gather.5.cloned.1.call-done) | copy-start | bytes 3145732
  110.7 5.2 %copy-start.20 = (bf16[512,256]{0,1:T(8,128)(2,1)}, bf16[512,256]{0,1:T(8,128)(2,1)S(1)}, u32[]{:S(2)}) copy-start(bf16[512,256]{0,1:T(8,128)(2,1)S(1)} %copy.62) | copy-start | bytes 786436
  110.9 5.1 %copy-start.21 = (bf16[512,256]{0,1:T(8,128)(2,1)}, bf16[512,256]{0,1:T(8,128)(2,1)S(1)}, u32[]{:S(2)}) copy-start(bf16[512,256]{0,1:T(8,128)(2,1)S(1)} %copy.61) | copy-start | bytes 786436
  116.0 3.4 copy-start.26
  119.3 30.1 %copy-start.13 = (bf16[4,64,512]{2,1,0:T(8,128)(2,1)}, bf16[4,64,512]{2,1,0:T(8,128)(2,1)S(1)}, u32[]{:S(2)}) copy-start(bf16[4,64,512]{2,1,0:T(8,128)(2,1)S(1)} %convolution_convert_fusion.10) | copy-start | bytes 786436
  119.4 26.0 %copy-start = (bf16[1,128,1024]{2,1,0:T(8,128)(2,1)S(1)}, bf16[1,128,1024]{2,1,0:T(8,128)(2,1)}, u32[]{:S(2)}) copy-start(bf16[1,128,1024]{2,1,0:T(8,128)(2,1)} %param.19) | copy-start | bytes 786436
  120.8 55.4 %all-gather.9.cloned.1.call-start = ((), (), s32[]{:S(2)}) async-start(), calls=%async_computation.11 | async-start | bytes 1310720 | tf_op jit(solution)/shard_map/all_gather | solution.py:419
  149.5 63.4 %reduce-scatter.7.cloned.1.call-start = ((), (), s32[]{:S(2)}) async-start(), calls=%async_computation.12 | async-start | bytes 1310720 | tf_op jit(solution)/shard_map/reduce_scatter | solution.py:426
  176.2 3.3 copy-start.38
  176.2 3.3 copy-start.42
  179.6 3.3 copy-start.45
  179.6 4.3 %copy-start.40 = (bf16[4,4,64,1024]{3,2,1,0:T(8,128)(2,1)S(1)}, bf16[4,4,64,1024]{3,2,1,0:T(8,128)(2,1)}, u32[]{:S(2)}) copy-start(bf16[4,4,64,1024]{3,2,1,0:T(8,128)(2,1)} %get-tuple-element.44) | copy-start | bytes 6291460
  183.8 29.1 %copy-start.1 = (bf16[128,1024]{1,0:T(8,128)(2,1)S(1)}, bf16[128,1024]{1,0:T(8,128)(2,1)}, u32[]{:S(2)}) copy-start(bf16[128,1024]{1,0:T(8,128)(2,1)} %reduce-scatter.5.cloned.1.call-done) | copy-start | bytes 786436
  186.1 29.4 %copy-start.12 = (bf16[1,128,1024]{2,1,0:T(8,128)(2,1)S(1)}, bf16[1,128,1024]{2,1,0:T(8,128)(2,1)}, u32[]{:S(2)}) copy-start(bf16[1,128,1024]{2,1,0:T(8,128)(2,1)} %param.20) | copy-start | bytes 786436
  186.1 76.0 %all-gather.11.cloned.1.call-start = ((), (), s32[]{:S(2)}) async-start(), calls=%async_computation.13 | async-start | bytes 1310720 | tf_op jit(solution)/shard_map/all_gather | solution.py:434
  215.5 3.9 %copy-start.2 = (f32[128,1024]{1,0:T(8,128)}, f32[128,1024]{1,0:T(8,128)S(1)}, u32[]{:S(2)}) copy-start(f32[128,1024]{1,0:T(8,128)S(1)} %get-tuple-element.78) | copy-start | bytes 1572868
  216.4 3.0 copy-start.43
  216.4 3.0 copy-start.46
  251.8 27.1 %all-to-all-start.2 = ((bf16[4,64,1024]{2,1,0:T(8,128)(2,1)}), bf16[4,64,1024]{2,1,0:T(8,128)(2,1)S(1)}, u32[]{:S(2)}, u32[]{:S(2)}) async-start(bf16[4,64,1024]{2,1,0:T(8,128)(2,1)} %get-tuple-element.51), calls=%async_computation.6 | async-start | bytes 1048576 | tf_op jit(solution)/shard_map/all_to_all | solution.py:518
  255.3 69.2 %reduce-scatter.11.cloned.1.call-start = ((), (), s32[]{:S(2)}) async-start(), calls=%async_computation.15 | async-start | bytes 1310720 | tf_op jit(solution)/shard_map/reduce_scatter | solution.py:477
  255.6 4.0 %copy-start.39 = (bf16[4,4,64,1024]{3,2,1,0:T(8,128)(2,1)S(1)}, bf16[4,4,64,1024]{3,2,1,0:T(8,128)(2,1)}, u32[]{:S(2)}) copy-start(bf16[4,4,64,1024]{3,2,1,0:T(8,128)(2,1)} %get-tuple-element.46) | copy-start | bytes 6291460
  255.6 4.0 %copy-start.47 = (f32[512,1024]{1,0:T(8,128)S(1)}, f32[512,1024]{1,0:T(8,128)}, u32[]{:S(2)}) copy-start(f32[512,1024]{1,0:T(8,128)} %copy-done.45) | copy-start | bytes 6291460
  259.6 2.5 copy-start.27
  259.6 4.2 %copy-start.31 = (bf16[512,256]{0,1:T(8,128)(2,1)S(1)}, bf16[512,256]{0,1:T(8,128)(2,1)}, u32[]{:S(2)}) copy-start(bf16[512,256]{0,1:T(8,128)(2,1)} %copy.60) | copy-start | bytes 786436
  263.9 3.1 copy-start.44
  263.9 3.5 %copy-start.4 = (f32[4,512,512]{1,2,0:T(8,128)S(1)}, f32[4,512,512]{1,2,0:T(8,128)}, u32[]{:S(2)}) copy-start(f32[4,512,512]{1,2,0:T(8,128)} %get-tuple-element.96) | copy-start | bytes 12582916
  274.5 2.3 copy-start.15
  274.5 2.3 copy-start.28
  274.5 2.3 copy-start.41
  282.0 24.6 %copy-start.6 = (f32[64,4096]{1,0:T(8,128)S(1)}, f32[64,4096]{1,0:T(8,128)}, u32[]{:S(2)}) copy-start(f32[64,4096]{1,0:T(8,128)} %param.25) | copy-start | bytes 3145732
  301.6 17.3 %all-to-all-start.1 = ((bf16[4,64,768]{2,1,0:T(8,128)(2,1)}), bf16[4,64,768]{2,1,0:T(8,128)(2,1)}, u32[]{:S(2)}, u32[]{:S(2)}) async-start(bf16[4,64,768]{2,1,0:T(8,128)(2,1)} %get-tuple-element.49), calls=%async_computation.5 | async-start | bytes 786432 | tf_op jit(solution)/shard_map/all_to_all | solution.py:522
  306.7 33.9 %reduce-scatter.9.cloned.1.call-start = ((), (), s32[]{:S(2)}) async-start(), calls=%async_computation.14 | async-start | bytes 1310720 | tf_op jit(solution)/shard_map/reduce_scatter | solution.py:438
  306.7 3.8 %copy-start.11 = (bf16[128,1024]{1,0:T(8,128)(2,1)S(1)}, bf16[128,1024]{1,0:T(8,128)(2,1)}, u32[]{:S(2)}) copy-start(bf16[128,1024]{1,0:T(8,128)(2,1)} %reduce-scatter.7.cloned.1.call-done) | copy-start | bytes 786436
  310.5 1.8 copy-start.32
  310.5 1.8 copy-start.33
  313.3 8.0 %copy-start.10 = (f32[64,3072]{1,0:T(8,128)S(1)}, f32[64,3072]{1,0:T(8,128)}, u32[]{:S(2)}) copy-start(f32[64,3072]{1,0:T(8,128)} %param.23) | copy-start | bytes 2359300
  324.5 16.1 %copy-start.3 = (f32[128,1024]{1,0:T(8,128)S(1)}, f32[128,1024]{1,0:T(8,128)}, u32[]{:S(2)}) copy-start(f32[128,1024]{1,0:T(8,128)} %copy-done.2) | copy-start | bytes 1572868
  325.6 18.4 %copy-start.34 = (f32[832]{0:T(1024)S(1)}, f32[832]{0:T(1024)}, u32[]{:S(2)}) copy-start(f32[832]{0:T(1024)} %param.27) | copy-start | bytes 9988
  325.6 18.4 %copy-start.36 = (f32[832]{0:T(1024)S(1)}, f32[832]{0:T(1024)}, u32[]{:S(2)}) copy-start(f32[832]{0:T(1024)} %param.32) | copy-start | bytes 9988
  325.6 18.4 %copy-start.37 = (f32[832]{0:T(1024)S(1)}, f32[832]{0:T(1024)}, u32[]{:S(2)}) copy-start(f32[832]{0:T(1024)} %param.37) | copy-start | bytes 9988
  335.1 8.8 %all-to-all-start.3 = ((bf16[4,16,128]{2,1,0:T(8,128)(2,1)}), bf16[4,16,128]{2,1,0:T(8,128)(2,1)S(1)}, u32[]{:S(2)}, u32[]{:S(2)}) async-start(bf16[4,16,128]{2,1,0:T(8,128)(2,1)} %shard_map.317), calls=%async_computation.7 | async-start | bytes 32768 | tf_op jit(solution)/shard_map/all_to_all | solution.py:523
  (12 other events, 16.3 us)
Sparse Core Ops, SparseCore 0:
  44.6 27.0 all-gather.4
  73.3 27.4 all-gather.6
  121.0 24.3 reduce-scatter.4
  149.6 26.5 all-gather.8
  186.3 26.6 reduce-scatter.6
  216.5 26.5 all-gather.10
  279.0 28.3 reduce-scatter.10
  312.4 28.1 reduce-scatter.8
